TPU v7x, 256 devices: a whole 4x4x8 slice. The times are simulated.
256 devices in a mesh: th: 16 (over z_hi, y), tw: 16 (over z_lo, x, core).
Axes of the slice: x: 4, y: 4, z: 8 (z_hi: 4, z_lo: 2; z = z_hi * 2 + z_lo), core: 2. Of those that a mesh axis runs over, the one named last changes fastest.
Arguments:
- query_vectors: bfloat16 [2, 128, 128, 1536], P(None, 'th', 'tw'), may hold values from -6 to 6
- key_vectors: bfloat16 [2, 128, 128, 1536], P(None, 'th', 'tw'), may hold values from -6 to 6
- value_vectors: bfloat16 [2, 128, 128, 1536], P(None, 'th', 'tw'), may hold values from -6 to 6
- out_grad: bfloat16 [2, 128, 128, 3072], P(None, 'th', 'tw'), may hold values from -6 to 6
- out_weight: bfloat16 [1536, 3072], P(('th', 'tw')), may hold values from -0.4375 to 0.4375
- window_extent: int32 [2, 12], replicated, may hold values from 0 to 1, as said below
- edge_pad: int32 [2], replicated, may hold values from 1 to 7, as said below
Outputs:
- block_output: bfloat16 [2, 128, 128, 3072], P(None, 'th', 'tw')
- grad_queries: bfloat16 [2, 128, 128, 1536], P(None, 'th', 'tw')
- grad_keys: bfloat16 [2, 128, 128, 1536], P(None, 'th', 'tw')
- grad_values: bfloat16 [2, 128, 128, 1536], P(None, 'th', 'tw')
Inputs may be any that keep to these rules, and one draw needn't show every extreme that they name: `window_extent`: in each of the two rows some head has 0 and some head has 1. `edge_pad`: one of the two entries is 7.
All inputs are finite; a program needn't handle non-finite values.
Results may differ from a plain program's by a relative error of at most 0.018.
Values may be sent and summed in bfloat16 or wider, within the bound.
A program may use at most 192 MiB of HBM per device.

v0:
```python
import jax
import jax.numpy as jnp
from jax import lax
from jax.sharding import PartitionSpec as P

masked_score = -1e30


def extended(shard, sides, width):
    for axis, dim in sides:
        size, length = (lax.axis_size(axis), shard.shape[dim])
        up = [(i, (i + 1) % size) for i in range(size - 1)]
        down = [(j, i) for i, j in up]
        last = lax.slice_in_dim(shard, length - width, length, axis=dim)
        initial = lax.slice_in_dim(shard, 0, width, axis=dim)
        before = lax.ppermute(last, axis, up)
        after = lax.ppermute(initial, axis, down)
        shard = jnp.concatenate([before, shard, after], axis=dim)
    return shard


def window_mask(extent, tile_size, frames):
    offsets = jnp.arange(3 * tile_size, dtype=jnp.int32) // tile_size - 1
    distance = jnp.abs(offsets)
    inside = (distance[None, :, None] <= extent[0][:, None, None]) & (
        distance[None, None, :] <= extent[1][:, None, None]
    )
    head_count = extent.shape[1]
    inside = jnp.broadcast_to(inside[:, None], (head_count, frames, 3 * tile_size, 3 * tile_size))
    return inside.reshape(head_count, frames * 9 * tile_size * tile_size)


def cell_valid(row_start, col_start, span_cells, frames, limit_rows, limit_cols):
    row_ids = row_start + jnp.arange(span_cells, dtype=jnp.int32)
    col_ids = col_start + jnp.arange(span_cells, dtype=jnp.int32)
    inside = ((row_ids >= 0) & (row_ids < limit_rows))[:, None] & (
        (col_ids >= 0) & (col_ids < limit_cols)
    )[None, :]
    return jnp.broadcast_to(inside[None], (frames, span_cells, span_cells)).reshape(-1)


def on_device(
    query_vectors, key_vectors, value_vectors, out_grad, out_weight, window_extent, edge_pad
):
    frames = query_vectors.shape[0]
    tile_size = query_vectors.shape[1]
    feature_width = query_vectors.shape[3]
    head_count = window_extent.shape[1]
    head_size = feature_width // head_count
    model_width = out_grad.shape[3]
    factor = head_size ** (-0.5)
    cells_tile = frames * tile_size * tile_size
    limit_rows = tile_size * lax.axis_size("th") - edge_pad[0]
    limit_cols = tile_size * lax.axis_size("tw") - edge_pad[1]
    row_start = lax.axis_index("th") * tile_size - tile_size
    col_start = lax.axis_index("tw") * tile_size - tile_size
    in_window = window_mask(window_extent, tile_size, frames)
    key_allowed = (
        in_window
        & cell_valid(row_start, col_start, 3 * tile_size, frames, limit_rows, limit_cols)[None, :]
    )
    own_valid = cell_valid(
        row_start + tile_size, col_start + tile_size, tile_size, frames, limit_rows, limit_cols
    )

    def split_heads(block):
        return block.reshape(-1, head_count, head_size)

    own_queries = split_heads(query_vectors)
    near_keys, near_values = (
        extended(key_vectors, (("th", 1), ("tw", 2)), tile_size),
        extended(value_vectors, (("th", 1), ("tw", 2)), tile_size),
    )
    near_keys = split_heads(near_keys)
    near_values = split_heads(near_values)
    scores = (
        jnp.einsum("qhd,khd->hqk", own_queries, near_keys, preferred_element_type=jnp.float32)
        * factor
    )
    scores = jnp.where(key_allowed[:, None, :], scores, masked_score)
    highest = jnp.max(scores, axis=2, keepdims=True)
    raised = jnp.exp(scores - highest)
    summed = jnp.sum(raised, axis=2, keepdims=True)
    log_total = highest + jnp.log(summed)
    probabilities = (raised / summed).astype(jnp.bfloat16)
    attended = jnp.einsum(
        "hqk,khd->qhd", probabilities, near_values, preferred_element_type=jnp.float32
    )
    attended = attended.astype(jnp.bfloat16).reshape(cells_tile, feature_width)
    grad_rows = out_grad.reshape(cells_tile, model_width)
    weight_rows = lax.all_gather(out_weight, ("th", "tw"), axis=0, tiled=True)
    partial_sum = jnp.dot(attended, weight_rows, preferred_element_type=jnp.float32)
    grads_part = lax.dot_general(
        grad_rows, weight_rows, (((1,), (1,)), ((), ())), preferred_element_type=jnp.float32
    )
    grad_columns = grads_part.astype(jnp.bfloat16)
    block_output = partial_sum.astype(jnp.bfloat16).reshape(
        frames, tile_size, tile_size, model_width
    )
    d_heads = split_heads(grad_columns)
    correction = jnp.sum(
        split_heads(attended).astype(jnp.float32) * d_heads.astype(jnp.float32), axis=2
    )
    correction_heads = correction.T[:, :, None]
    weights = jnp.where(key_allowed[:, None, :], jnp.exp(scores - log_total), 0.0)
    d_probs = jnp.einsum("qhd,khd->hqk", d_heads, near_values, preferred_element_type=jnp.float32)
    d_scores = (weights * (d_probs - correction_heads)).astype(jnp.bfloat16)
    grad_queries = (
        jnp.einsum("hqk,khd->qhd", d_scores, near_keys, preferred_element_type=jnp.float32) * factor
    )
    grad_queries = grad_queries.astype(jnp.bfloat16).reshape(
        frames, tile_size, tile_size, feature_width
    )
    near_queries, near_grads = (
        extended(query_vectors, (("th", 1), ("tw", 2)), tile_size),
        extended(
            grad_columns.reshape(frames, tile_size, tile_size, feature_width),
            (("th", 1), ("tw", 2)),
            tile_size,
        ),
    )
    total_cells = log_total[:, :, 0].T.reshape(frames, tile_size, tile_size, head_count)
    correction_cells = correction.reshape(frames, tile_size, tile_size, head_count)
    near_totals, near_corrections = (
        extended(total_cells, (("th", 1), ("tw", 2)), tile_size),
        extended(correction_cells, (("th", 1), ("tw", 2)), tile_size),
    )
    near_queries = split_heads(near_queries)
    near_grads = split_heads(near_grads)
    near_totals = near_totals.reshape(-1, head_count).T[:, :, None]
    near_corrections = near_corrections.reshape(-1, head_count).T[:, :, None]
    query_allowed = in_window[:, :, None] & own_valid[None, None, :]
    back_scores = (
        jnp.einsum(
            "qhd,khd->hqk",
            near_queries,
            split_heads(key_vectors),
            preferred_element_type=jnp.float32,
        )
        * factor
    )
    back_weights = jnp.where(query_allowed, jnp.exp(back_scores - near_totals), 0.0)
    back_probs = jnp.einsum(
        "qhd,khd->hqk", near_grads, split_heads(value_vectors), preferred_element_type=jnp.float32
    )
    back_dscores = (back_weights * (back_probs - near_corrections)).astype(jnp.bfloat16)
    grad_keys = (
        jnp.einsum("hqk,qhd->khd", back_dscores, near_queries, preferred_element_type=jnp.float32)
        * factor
    )
    grad_values = jnp.einsum(
        "hqk,qhd->khd",
        back_weights.astype(jnp.bfloat16),
        near_grads,
        preferred_element_type=jnp.float32,
    )
    grad_keys = grad_keys.astype(jnp.bfloat16).reshape(frames, tile_size, tile_size, feature_width)
    grad_values = grad_values.astype(jnp.bfloat16).reshape(
        frames, tile_size, tile_size, feature_width
    )
    return (block_output, grad_queries, grad_keys, grad_values)


def solution(mesh):
    in_specs = (
        P(None, "th", "tw", None),
        P(None, "th", "tw", None),
        P(None, "th", "tw", None),
        P(None, "th", "tw", None),
        P(("th", "tw"), None),
        P(),
        P(),
    )
    out_specs = (
        P(None, "th", "tw", None),
        P(None, "th", "tw", None),
        P(None, "th", "tw", None),
        P(None, "th", "tw", None),
    )
    return jax.shard_map(
        on_device, mesh=mesh, in_specs=in_specs, out_specs=out_specs, check_vma=False
    )
```

profile of v0, /device:TPU:1, one launch (start us, length us, event | category | flops | bytes accessed | tf_op | source)
XLA Modules:
  0.0 573.9 jit_solution(14943674017081210330)
XLA Ops:
  7.9 4.8 collective-permute-start.4
  14.0 4.0 collective-permute-start
  19.4 4.0 collective-permute-start.8
  23.4 2.1 reshape.290
  25.5 2.1 reshape.297
  27.6 2.1 reshape.302
  31.3 1.7 reshape.288
  33.0 1.3 fusion.43
  36.0 1.3 broadcast_and_fusion.1
  39.8 4.0 collective-permute-start.7
  44.5 3.0 collective-permute-start.6
  48.6 1.9 collective-permute-start.3
  51.3 3.6 collective-permute-start.2
  56.1 1.9 collective-permute-start.11
  58.0 1.7 collective-permute-done.7
  59.7 2.0 collective-permute-start.10
  61.7 1.9 pad_maximum_fusion.1
  63.6 7.4 %reshape.289 = bf16[1152,12,128]{2,1,0:T(8,128)(2,1)} reshape(bf16[2,24,24,1536]{3,2,1,0:T(8,128)(2,1)} %pad_maximum_fusion.1) | data formatting | bytes 7077888 | tf_op jit(solution)/shard_map/reshape | solution.py:67
  71.0 6.9 %copy.70 = bf16[1152,12,128]{0,2,1:T(8,128)(2,1)} copy(bf16[1152,12,128]{2,1,0:T(8,128)(2,1)} %reshape.289) | data formatting | bytes 7077888 | tf_op jit(solution)/shard_map/reshape | solution.py:67
  77.9 5.7 %bitcast_reduce_fusion = (f32[12,128]{1,0:T(8,128)S(1)}, f32[12,1152,128]{2,1,0:T(8,128)S(1)}) fusion(bf16[1152,12,128]{0,2,1:T(8,128)(2,1)} %copy.70, bf16[128,12,128]{2,1,0:T(8,128)(2,1)} %reshape.290, pred[12,1152]{1,0:T(8,128)(4,1)S(1)} %copy-done.11), kind=kOutput, calls=%fused_computation.2 | convolution fusion | flops 458291712 | bytes 11030016 | tf_op jit(solution)/shard_map/qhd,khd->hqk/dot_general | solution.py:77
  84.6 1.9 copy-done.2
  87.9 4.9 collective-permute-start.12
  92.8 3.1 pad_maximum_fusion
  96.4 3.0 collective-permute-start.15
  99.4 3.1 collective-permute-start.14
  102.6 3.1 pad_maximum_fusion.2
  105.7 7.4 %reshape.287 = bf16[1152,12,128]{2,1,0:T(8,128)(2,1)} reshape(bf16[2,24,24,1536]{3,2,1,0:T(8,128)(2,1)} %pad_maximum_fusion) | data formatting | bytes 7077888 | tf_op jit(solution)/shard_map/reshape | solution.py:67
  113.1 7.4 %reshape.296 = bf16[1152,12,128]{2,1,0:T(8,128)(2,1)} reshape(bf16[2,24,24,1536]{3,2,1,0:T(8,128)(2,1)} %pad_maximum_fusion.2) | data formatting | bytes 7077888 | tf_op jit(solution)/shard_map/reshape | solution.py:67
  120.5 7.0 %copy.85 = bf16[1152,12,128]{0,2,1:T(8,128)(2,1)} copy(bf16[1152,12,128]{2,1,0:T(8,128)(2,1)} %reshape.296) | data formatting | bytes 7077888 | tf_op jit(solution)/shard_map/reshape | solution.py:67
  128.0 8.6 %exponential_select_fusion = f32[12,1152,128]{2,1,0:T(8,128)} fusion(bf16[1152,12,128]{0,2,1:T(8,128)(2,1)} %copy.85, f32[12,1152]{1,0:T(8,128)S(1)} %bitcast.105, pred[128]{0:T(512)(128)(4,1)S(1)} %and.151, pred[12,1152]{1,0:T(8,128)(4,1)S(1)} %copy-done.10, bf16[128,12,128]{2,1,0:T(8,128)(2,1)S(1)} %copy-done.7), kind=kOutput, calls=%fused_computation.9 | convolution fusion | flops 460062720 | bytes 11079296 | tf_op jit(solution)/shard_map/qhd,khd->hqk/dot_general | solution.py:134
  136.6 325.1 %all-gather.3.cloned.1.call-done = bf16[256,6,3072]{2,1,0:T(8,128)(2,1)} async-done(((bf16[1,6,3072]{2,1,0:T(8,128)(2,1)}), bf16[256,6,3072]{2,1,0:T(8,128)(2,1)}) %all-gather.3.cloned.1.call-update) | async-done | bytes 9437200 | tf_op jit(solution)/shard_map/all_gather | solution.py:91
  461.8 14.2 %reshape.308 = bf16[1536,3072]{1,0:T(8,128)(2,1)} reshape(bf16[256,6,3072]{2,1,0:T(8,128)(2,1)} %all-gather.3.cloned.1.call-done) | data formatting | bytes 18874368
  475.9 6.9 %convolution_convert_fusion.1 = bf16[128,1536]{1,0:T(8,128)(2,1)S(1)} fusion(bf16[128,3072]{1,0:T(8,128)(2,1)S(1)} %bitcast.95, bf16[1536,3072]{1,0:T(8,128)(2,1)} %reshape.308), kind=kOutput, calls=%fused_computation.23 | convolution fusion | flops 1208156160 | bytes 10616832 | tf_op jit(solution)/shard_map/dot_general | solution.py:93
  484.4 4.0 collective-permute-start.16
  488.4 7.3 %multiply_reduce_fusion = (f32[128,12]{0,1:T(8,128)S(1)}, bf16[12,128,128]{2,1,0:T(8,128)(2,1)S(1)}) fusion(bf16[128,12,128]{0,2,1:T(8,128)(2,1)S(1)} %bitcast.102, f32[12,1152,128]{2,1,0:T(8,128)} %copy-done.2, f32[12,128]{1,0:T(8,128)S(1)} %fusion.5, f32[12,128]{1,0:T(8,128)S(1)} %get-tuple-element.14, bf16[1152,12,128]{2,1,0:T(8,128)(2,1)} %reshape.287), kind=kOutput, calls=%fused_computation.36 | convolution fusion | flops 459274752 | bytes 11421696 | tf_op jit(solution)/shard_map/hqk,khd->qhd/dot_general | solution.py:86
  497.1 4.0 collective-permute-start.20
  502.3 6.1 %collective-permute-start.19 = (bf16[2,24,8,1536]{3,2,1,0:T(8,128)(2,1)}, bf16[2,24,8,1536]{3,2,1,0:T(8,128)(2,1)S(1)}, u32[]{:S(2)}, u32[]{:S(2)}) collective-permute-start(bf16[2,24,8,1536]{3,2,1,0:T(8,128)(2,1)} %pad_maximum_fusion.4), channel_id=1, source_target_pairs={{1,0},{2,1},{3,2},{4,3},{5,4},{6,5},{7,6},{8,7},{9,8},{10,9},{11,1... | collective-permute-start | bytes 3538952 | tf_op jit(solution)/shard_map/ppermute | solution.py:17
  508.4 1.9 collective-permute-start.18
  510.3 9.3 %fusion.29 = bf16[128,12,128]{0,2,1:T(8,128)(2,1)} fusion(bf16[1152,12,128]{0,2,1:T(8,128)(2,1)} %copy.70, f32[12,1152,128]{2,1,0:T(8,128)} %copy-done.2, bf16[128,12,128]{0,2,1:T(8,128)(2,1)S(1)} %bitcast.103, f32[12,128]{1,0:T(8,128)S(1)} %bitcast.108, f32[12,128]{1,0:T(8,128)S(1)} %log_add_fusion, pred[12,1152]{1,0:T(8,128)(4,1)S(1)} %copy-done.11, ...), kind=kOutput, calls=%fused_computation.32 | convolution fusion | flops 915210240 | bytes 14968320 | tf_op jit(solution)/shard_map/hqk,khd->qhd/dot_general | solution.py:109
  520.1 3.6 collective-permute-start.23
  523.8 2.1 collective-permute-start.22
  525.9 6.0 %convolution_convert_fusion = bf16[128,3072]{1,0:T(8,128)(2,1)} fusion(bf16[128,1536]{0,1:T(8,128)(2,1)S(1)} %bitcast.100, bf16[1536,3072]{1,0:T(8,128)(2,1)} %reshape.308), kind=kOutput, calls=%fused_computation.13 | convolution fusion | flops 1208352768 | bytes 10616832 | tf_op jit(solution)/shard_map/dot_general | solution.py:92
  531.9 1.4 copy.72
  534.8 3.0 pad_maximum_fusion.3
  537.8 7.4 %reshape.301 = bf16[1152,12,128]{2,1,0:T(8,128)(2,1)} reshape(bf16[2,24,24,1536]{3,2,1,0:T(8,128)(2,1)} %pad_maximum_fusion.3) | data formatting | bytes 7077888 | tf_op jit(solution)/shard_map/reshape | solution.py:67
  545.1 6.9 %copy.87 = bf16[1152,12,128]{0,2,1:T(8,128)(2,1)} copy(bf16[1152,12,128]{2,1,0:T(8,128)(2,1)} %reshape.301) | data formatting | bytes 7077888 | tf_op jit(solution)/shard_map/reshape | solution.py:67
  552.1 5.2 fusion.32
  557.3 6.8 %fusion.35 = bf16[128,12,128]{0,2,1:T(8,128)(2,1)S(1)} fusion(bf16[1152,12,128]{0,2,1:T(8,128)(2,1)} %copy.85, f32[12,1152,128]{2,1,0:T(8,128)} %exponential_select_fusion, bf16[1152,12,128]{0,2,1:T(8,128)(2,1)} %copy.87, f32[12,1152]{1,0:T(8,128)S(1)} %bitcast.104, bf16[128,12,128]{2,1,0:T(8,128)(2,1)S(1)} %copy-done.3), kind=kOutput, calls=%fused_computation.34 | convolution fusion | flops 911671296 | bytes 14997504 | tf_op jit(solution)/shard_map/hqk,qhd->khd/dot_general | solution.py:148
  (101 shorter events, 23.3 us)
Async XLA Ops:
  7.2 468.8 %copy-start = (bf16[2,8,8,3072]{3,2,1,0:T(8,128)(2,1)S(1)}, bf16[2,8,8,3072]{3,2,1,0:T(8,128)(2,1)}, u32[]{:S(2)}) copy-start(bf16[2,8,8,3072]{3,2,1,0:T(8,128)(2,1)} %param.10) | copy-start | bytes 2359300
  7.2 32.5 %copy-start.4 = (bf16[2,8,8,1536]{3,2,1,0:T(8,128)(2,1)S(1)}, bf16[2,8,8,1536]{3,2,1,0:T(8,128)(2,1)}, u32[]{:S(2)}) copy-start(bf16[2,8,8,1536]{3,2,1,0:T(8,128)(2,1)} %param.8) | copy-start | bytes 1179652
  7.2 41.4 %copy-start.5 = (bf16[2,8,8,1536]{3,2,1,0:T(8,128)(2,1)S(1)}, bf16[2,8,8,1536]{3,2,1,0:T(8,128)(2,1)}, u32[]{:S(2)}) copy-start(bf16[2,8,8,1536]{3,2,1,0:T(8,128)(2,1)} %param.9) | copy-start | bytes 1179652
  7.2 454.6 %all-gather.3.cloned.1.call-start = ((), (), s32[]{:S(2)}) async-start(), calls=%async_computation | async-start | bytes 12632064 | tf_op jit(solution)/shard_map/all_gather | solution.py:91
  7.9 29.4 %collective-permute-start.4 = (bf16[2,8,8,1536]{3,2,1,0:T(8,128)(2,1)}, bf16[2,8,8,1536]{3,2,1,0:T(8,128)(2,1)}, u32[]{:S(2)}, u32[]{:S(2)}) collective-permute-start(bf16[2,8,8,1536]{3,2,1,0:T(8,128)(2,1)} %param.8), channel_id=1, source_target_pairs={{0,16},{16,32},{32,48},{48,64},{64,80},{80,96},{96,112},{112,128},... | collective-permute-start | bytes 1179656 | tf_op jit(solution)/shard_map/ppermute | solution.py:16
  12.8 27.0 %collective-permute-start.5 = (bf16[2,8,8,1536]{3,2,1,0:T(8,128)(2,1)}, bf16[2,8,8,1536]{3,2,1,0:T(8,128)(2,1)S(1)}, u32[]{:S(2)}, u32[]{:S(2)}) collective-permute-start(bf16[2,8,8,1536]{3,2,1,0:T(8,128)(2,1)} %param.8), channel_id=1, source_target_pairs={{16,0},{32,16},{48,32},{64,48},{80,64},{96,80},{112,96},{128,112},... | collective-permute-start | bytes 1179656 | tf_op jit(solution)/shard_map/ppermute | solution.py:17
  14.0 29.7 %collective-permute-start = (bf16[2,8,8,1536]{3,2,1,0:T(8,128)(2,1)}, bf16[2,8,8,1536]{3,2,1,0:T(8,128)(2,1)S(1)}, u32[]{:S(2)}, u32[]{:S(2)}) collective-permute-start(bf16[2,8,8,1536]{3,2,1,0:T(8,128)(2,1)} %param.9), channel_id=1, source_target_pairs={{0,16},{16,32},{32,48},{48,64},{64,80},{80,96},{96,112},{112,128},... | collective-permute-start | bytes 1179656 | tf_op jit(solution)/shard_map/ppermute | solution.py:16
  18.1 30.5 %collective-permute-start.1 = (bf16[2,8,8,1536]{3,2,1,0:T(8,128)(2,1)}, bf16[2,8,8,1536]{3,2,1,0:T(8,128)(2,1)S(1)}, u32[]{:S(2)}, u32[]{:S(2)}) collective-permute-start(bf16[2,8,8,1536]{3,2,1,0:T(8,128)(2,1)} %param.9), channel_id=1, source_target_pairs={{16,0},{32,16},{48,32},{64,48},{80,64},{96,80},{112,96},{128,112},... | collective-permute-start | bytes 1179656 | tf_op jit(solution)/shard_map/ppermute | solution.py:17
  19.4 31.2 %collective-permute-start.8 = (bf16[2,8,8,1536]{3,2,1,0:T(8,128)(2,1)}, bf16[2,8,8,1536]{3,2,1,0:T(8,128)(2,1)S(1)}, u32[]{:S(2)}, u32[]{:S(2)}) collective-permute-start(bf16[2,8,8,1536]{3,2,1,0:T(8,128)(2,1)} %param.7), channel_id=1, source_target_pairs={{0,16},{16,32},{32,48},{48,64},{64,80},{80,96},{96,112},{112,128},... | collective-permute-start | bytes 1179656 | tf_op jit(solution)/shard_map/ppermute | solution.py:16
  27.6 28.4 %copy-start.6 = (bf16[2,8,8,1536]{3,2,1,0:T(8,128)(2,1)S(1)}, bf16[2,8,8,1536]{3,2,1,0:T(8,128)(2,1)}, u32[]{:S(2)}) copy-start(bf16[2,8,8,1536]{3,2,1,0:T(8,128)(2,1)} %param.7) | copy-start | bytes 1179652
  37.4 18.7 %collective-permute-start.9 = (bf16[2,8,8,1536]{3,2,1,0:T(8,128)(2,1)}, bf16[2,8,8,1536]{3,2,1,0:T(8,128)(2,1)S(1)}, u32[]{:S(2)}, u32[]{:S(2)}) collective-permute-start(bf16[2,8,8,1536]{3,2,1,0:T(8,128)(2,1)} %param.7), channel_id=1, source_target_pairs={{16,0},{32,16},{48,32},{64,48},{80,64},{96,80},{112,96},{128,112},... | collective-permute-start | bytes 1179656 | tf_op jit(solution)/shard_map/ppermute | solution.py:17
  39.8 20.0 %collective-permute-start.7 = (bf16[2,24,8,1536]{3,2,1,0:T(8,128)(2,1)S(1)}, bf16[2,24,8,1536]{3,2,1,0:T(8,128)(2,1)S(1)}, u32[]{:S(2)}, u32[]{:S(2)}) collective-permute-start(bf16[2,24,8,1536]{3,2,1,0:T(8,128)(2,1)S(1)} %constant_dynamic-update-slice_fusion.3), channel_id=1, source_target_pairs={{1,0},{2,1},{3,2},{4,3},{5,4},{6,5},{7,6},{8,7},{9,8},{10,9},{11,1... | collective-permute-start | bytes 3538952 | tf_op jit(solution)/shard_map/ppermute | solution.py:17
  43.8 0.7 copy-start.9
  44.5 17.2 %collective-permute-start.6 = (bf16[2,24,8,1536]{3,2,1,0:T(8,128)(2,1)S(1)}, bf16[2,24,8,1536]{3,2,1,0:T(8,128)(2,1)S(1)}, u32[]{:S(2)}, u32[]{:S(2)}) collective-permute-start(bf16[2,24,8,1536]{3,2,1,0:T(8,128)(2,1)S(1)} %constant_dynamic-update-slice_fusion.3), channel_id=1, source_target_pairs={{0,1},{1,2},{2,3},{3,4},{4,5},{5,6},{6,7},{7,8},{8,9},{9,10},{10,1... | collective-permute-start | bytes 3538952 | tf_op jit(solution)/shard_map/ppermute | solution.py:16
  48.6 39.3 %collective-permute-start.3 = (bf16[2,24,8,1536]{3,2,1,0:T(8,128)(2,1)S(1)}, bf16[2,24,8,1536]{3,2,1,0:T(8,128)(2,1)}, u32[]{:S(2)}, u32[]{:S(2)}) collective-permute-start(bf16[2,24,8,1536]{3,2,1,0:T(8,128)(2,1)S(1)} %constant_dynamic-update-slice_fusion), channel_id=1, source_target_pairs={{1,0},{2,1},{3,2},{4,3},{5,4},{6,5},{7,6},{8,7},{9,8},{10,9},{11,1... | collective-permute-start | bytes 3538952 | tf_op jit(solution)/shard_map/ppermute | solution.py:17
  50.6 0.7 copy-start.8
  51.3 41.5 %collective-permute-start.2 = (bf16[2,24,8,1536]{3,2,1,0:T(8,128)(2,1)S(1)}, bf16[2,24,8,1536]{3,2,1,0:T(8,128)(2,1)}, u32[]{:S(2)}, u32[]{:S(2)}) collective-permute-start(bf16[2,24,8,1536]{3,2,1,0:T(8,128)(2,1)S(1)} %constant_dynamic-update-slice_fusion), channel_id=1, source_target_pairs={{0,1},{1,2},{2,3},{3,4},{4,5},{5,6},{6,7},{7,8},{8,9},{9,10},{10,1... | collective-permute-start | bytes 3538952 | tf_op jit(solution)/shard_map/ppermute | solution.py:16
  56.1 46.5 %collective-permute-start.11 = (bf16[2,24,8,1536]{3,2,1,0:T(8,128)(2,1)S(1)}, bf16[2,24,8,1536]{3,2,1,0:T(8,128)(2,1)}, u32[]{:S(2)}, u32[]{:S(2)}) collective-permute-start(bf16[2,24,8,1536]{3,2,1,0:T(8,128)(2,1)S(1)} %constant_dynamic-update-slice_fusion.6), channel_id=1, source_target_pairs={{1,0},{2,1},{3,2},{4,3},{5,4},{6,5},{7,6},{8,7},{9,8},{10,9},{11,1... | collective-permute-start | bytes 3538952 | tf_op jit(solution)/shard_map/ppermute | solution.py:17
  59.7 42.9 %collective-permute-start.10 = (bf16[2,24,8,1536]{3,2,1,0:T(8,128)(2,1)S(1)}, bf16[2,24,8,1536]{3,2,1,0:T(8,128)(2,1)}, u32[]{:S(2)}, u32[]{:S(2)}) collective-permute-start(bf16[2,24,8,1536]{3,2,1,0:T(8,128)(2,1)S(1)} %constant_dynamic-update-slice_fusion.6), channel_id=1, source_target_pairs={{0,1},{1,2},{2,3},{3,4},{4,5},{5,6},{6,7},{7,8},{8,9},{9,10},{10,1... | collective-permute-start | bytes 3538952 | tf_op jit(solution)/shard_map/ppermute | solution.py:16
  71.0 6.9 %copy-start.11 = (pred[12,1152]{1,0:T(8,128)(4,1)S(1)}, pred[12,1152]{1,0:T(8,128)(4,1)}, u32[]{:S(2)}) copy-start(pred[12,1152]{1,0:T(8,128)(4,1)} %broadcast_and_fusion.1) | copy-start | bytes 41476
  83.6 2.9 copy-start.2
  86.6 9.4 %collective-permute-start.13 = (f32[2,8,8,12]{2,1,0,3:T(8,128)S(1)}, f32[2,8,8,12]{2,1,0,3:T(8,128)S(1)}, u32[]{:S(2)}, u32[]{:S(2)}) collective-permute-start(f32[2,8,8,12]{2,1,0,3:T(8,128)S(1)} %reshape.298), channel_id=1, source_target_pairs={{16,0},{32,16},{48,32},{64,48},{80,64},{96,80},{112,96},{128,112},... | collective-permute-start | bytes 18440 | tf_op jit(solution)/shard_map/ppermute | solution.py:17
  87.9 8.2 %collective-permute-start.12 = (f32[2,8,8,12]{2,1,0,3:T(8,128)S(1)}, f32[2,8,8,12]{2,1,0,3:T(8,128)S(1)}, u32[]{:S(2)}, u32[]{:S(2)}) collective-permute-start(f32[2,8,8,12]{2,1,0,3:T(8,128)S(1)} %reshape.298), channel_id=1, source_target_pairs={{0,16},{16,32},{32,48},{48,64},{64,80},{80,96},{96,112},{112,128},... | collective-permute-start | bytes 18440 | tf_op jit(solution)/shard_map/ppermute | solution.py:16
  96.4 31.2 %collective-permute-start.15 = (f32[2,24,8,12]{1,2,3,0:T(8,128)S(1)}, f32[2,24,8,12]{1,2,3,0:T(8,128)S(1)}, u32[]{:S(2)}, u32[]{:S(2)}) collective-permute-start(f32[2,24,8,12]{1,2,3,0:T(8,128)S(1)} %pad_maximum_fusion.7), channel_id=1, source_target_pairs={{1,0},{2,1},{3,2},{4,3},{5,4},{6,5},{7,6},{8,7},{9,8},{10,9},{11,1... | collective-permute-start | bytes 55304 | tf_op jit(solution)/shard_map/ppermute | solution.py:17
  99.4 28.2 %collective-permute-start.14 = (f32[2,24,8,12]{1,2,3,0:T(8,128)S(1)}, f32[2,24,8,12]{1,2,3,0:T(8,128)S(1)}, u32[]{:S(2)}, u32[]{:S(2)}) collective-permute-start(f32[2,24,8,12]{1,2,3,0:T(8,128)S(1)} %pad_maximum_fusion.7), channel_id=1, source_target_pairs={{0,1},{1,2},{2,3},{3,4},{4,5},{5,6},{6,7},{7,8},{8,9},{9,10},{10,1... | collective-permute-start | bytes 55304 | tf_op jit(solution)/shard_map/ppermute | solution.py:16
  120.5 7.5 %copy-start.7 = (bf16[128,12,128]{2,1,0:T(8,128)(2,1)S(1)}, bf16[128,12,128]{2,1,0:T(8,128)(2,1)}, u32[]{:S(2)}) copy-start(bf16[128,12,128]{2,1,0:T(8,128)(2,1)} %reshape.297) | copy-start | bytes 1179652
  120.5 7.5 %copy-start.10 = (pred[12,1152]{1,0:T(8,128)(4,1)S(1)}, pred[12,1152]{1,0:T(8,128)(4,1)}, u32[]{:S(2)}) copy-start(pred[12,1152]{1,0:T(8,128)(4,1)} %reshape.288) | copy-start | bytes 41476
  483.1 18.1 %collective-permute-start.17 = (bf16[2,8,8,1536]{3,2,1,0:T(8,128)(2,1)S(1)}, bf16[2,8,8,1536]{3,2,1,0:T(8,128)(2,1)S(1)}, u32[]{:S(2)}, u32[]{:S(2)}) collective-permute-start(bf16[2,8,8,1536]{3,2,1,0:T(8,128)(2,1)S(1)} %bitcast.96), channel_id=1, source_target_pairs={{16,0},{32,16},{48,32},{64,48},{80,64},{96,80},{112,96},{128,112},... | collective-permute-start | bytes 1179656 | tf_op jit(solution)/shard_map/ppermute | solution.py:17
  484.4 16.8 %collective-permute-start.16 = (bf16[2,8,8,1536]{3,2,1,0:T(8,128)(2,1)S(1)}, bf16[2,8,8,1536]{3,2,1,0:T(8,128)(2,1)S(1)}, u32[]{:S(2)}, u32[]{:S(2)}) collective-permute-start(bf16[2,8,8,1536]{3,2,1,0:T(8,128)(2,1)S(1)} %bitcast.97), channel_id=1, source_target_pairs={{0,16},{16,32},{32,48},{48,64},{64,80},{80,96},{96,112},{112,128},... | collective-permute-start | bytes 1179656 | tf_op jit(solution)/shard_map/ppermute | solution.py:16
  495.8 23.9 %collective-permute-start.21 = (f32[2,8,8,12]{2,1,0,3:T(8,128)S(1)}, f32[2,8,8,12]{2,1,0,3:T(8,128)S(1)}, u32[]{:S(2)}, u32[]{:S(2)}) collective-permute-start(f32[2,8,8,12]{2,1,0,3:T(8,128)S(1)} %reshape.303), channel_id=1, source_target_pairs={{16,0},{32,16},{48,32},{64,48},{80,64},{96,80},{112,96},{128,112},... | collective-permute-start | bytes 18440 | tf_op jit(solution)/shard_map/ppermute | solution.py:17
  497.1 22.8 %collective-permute-start.20 = (f32[2,8,8,12]{2,1,0,3:T(8,128)S(1)}, f32[2,8,8,12]{2,1,0,3:T(8,128)S(1)}, u32[]{:S(2)}, u32[]{:S(2)}) collective-permute-start(f32[2,8,8,12]{2,1,0,3:T(8,128)S(1)} %reshape.303), channel_id=1, source_target_pairs={{0,16},{16,32},{32,48},{48,64},{64,80},{80,96},{96,112},{112,128},... | collective-permute-start | bytes 18440 | tf_op jit(solution)/shard_map/ppermute | solution.py:16
  502.3 32.5 %collective-permute-start.19 = (bf16[2,24,8,1536]{3,2,1,0:T(8,128)(2,1)}, bf16[2,24,8,1536]{3,2,1,0:T(8,128)(2,1)S(1)}, u32[]{:S(2)}, u32[]{:S(2)}) collective-permute-start(bf16[2,24,8,1536]{3,2,1,0:T(8,128)(2,1)} %pad_maximum_fusion.4), channel_id=1, source_target_pairs={{1,0},{2,1},{3,2},{4,3},{5,4},{6,5},{7,6},{8,7},{9,8},{10,9},{11,1... | collective-permute-start | bytes 3538952 | tf_op jit(solution)/shard_map/ppermute | solution.py:17
  508.4 26.4 %collective-permute-start.18 = (bf16[2,24,8,1536]{3,2,1,0:T(8,128)(2,1)}, bf16[2,24,8,1536]{3,2,1,0:T(8,128)(2,1)}, u32[]{:S(2)}, u32[]{:S(2)}) collective-permute-start(bf16[2,24,8,1536]{3,2,1,0:T(8,128)(2,1)} %pad_maximum_fusion.4), channel_id=1, source_target_pairs={{0,1},{1,2},{2,3},{3,4},{4,5},{5,6},{6,7},{7,8},{8,9},{9,10},{10,1... | collective-permute-start | bytes 3538952 | tf_op jit(solution)/shard_map/ppermute | solution.py:16
  520.1 14.2 %collective-permute-start.23 = (f32[2,24,8,12]{1,2,3,0:T(8,128)S(1)}, f32[2,24,8,12]{1,2,3,0:T(8,128)S(1)}, u32[]{:S(2)}, u32[]{:S(2)}) collective-permute-start(f32[2,24,8,12]{1,2,3,0:T(8,128)S(1)} %pad_maximum_fusion.8), channel_id=1, source_target_pairs={{1,0},{2,1},{3,2},{4,3},{5,4},{6,5},{7,6},{8,7},{9,8},{10,9},{11,1... | collective-permute-start | bytes 55304 | tf_op jit(solution)/shard_map/ppermute | solution.py:17
  523.8 10.6 %collective-permute-start.22 = (f32[2,24,8,12]{1,2,3,0:T(8,128)S(1)}, f32[2,24,8,12]{1,2,3,0:T(8,128)S(1)}, u32[]{:S(2)}, u32[]{:S(2)}) collective-permute-start(f32[2,24,8,12]{1,2,3,0:T(8,128)S(1)} %pad_maximum_fusion.8), channel_id=1, source_target_pairs={{0,1},{1,2},{2,3},{3,4},{4,5},{5,6},{6,7},{7,8},{8,9},{9,10},{10,1... | collective-permute-start | bytes 55304 | tf_op jit(solution)/shard_map/ppermute | solution.py:16
  552.1 5.2 copy-start.3
  557.3 9.8 %copy-start.1 = (bf16[2,8,8,3072]{3,2,1,0:T(8,128)(2,1)S(1)}, bf16[2,8,8,3072]{3,2,1,0:T(8,128)(2,1)}, u32[]{:S(2)}) copy-start(bf16[2,8,8,3072]{3,2,1,0:T(8,128)(2,1)} %param.10) | copy-start | bytes 2359300
Sparse Core Ops, SparseCore 0:
  9.9 451.7 all-gather.2
where the time goes:
time: 583 us; the launch traced here: 574 us
  waiting for transfers between devices  328 us (56%)
  local copies, waits for them, and re-layouts  89 us (15%)
  starting transfers between devices  69.9 us (12%)
  matrix products  56 us (10%)
  between operations  16 us (3%)
  other arithmetic  15.4 us (3%)
    all_gather x1, waiting for transfers between devices, on_device(): weight_rows = lax.all_gather(out_weight, ('th', 'tw'), axis=0, tiled=True)  325 us
    reshape x10, local copies, waits for them, and re-layouts, split_heads(): return block.reshape(-1, head_count, head_size)  56.7 us
    ppermute x12, starting transfers between devices, extended(): before = lax.ppermute(last, axis, up)  41.5 us
    ppermute x12, starting transfers between devices, extended(): after = lax.ppermute(initial, axis, down)  28.3 us
    unnamed x31, local copies, waits for them, and re-layouts  20.8 us
    concatenate x9, other arithmetic, extended(): shard = jnp.concatenate([before, shard, after], axis=dim)  12.8 us
  transfers between devices with their start and end apart: 25, of which 2 were waited for; matrix products, arithmetic and copies ran while one was open for 18% of the time, Pallas kernels for 0%

commit v1 on v0

v1 whole, which is shorter than its diff:
```python
import jax
import jax.numpy as jnp
from jax import lax
from jax.experimental import pallas as pl
from jax.experimental.pallas import tpu as pltpu
from jax.sharding import PartitionSpec as P

MESH = pl.DeviceIdType.MESH
HEADS, HD, TOK = 12, 128, 128
GROUPS, PER = 4, 3
D, E = 3072, 1536
SLABS = 8
SLABW = D // SLABS
OWN = 4
CELLS = 9 * TOK
MASKED = -1e30
FACTOR = HD ** (-0.5)
BF, F32 = jnp.bfloat16, jnp.float32


def nt(a, b):
    return lax.dot_general(a, b, (((1,), (1,)), ((), ())), preferred_element_type=F32)


def nn(a, b):
    return jnp.dot(a, b, preferred_element_type=F32)


def kernel(
    ext_ref, pad_ref, q_hbm, k_hbm, v_hbm, g_hbm, w_hbm,
    out_ref, dq_ref, dk_ref, dv_ref,
    qn, kn, vn, dn, wb, grads, pieces, block, att, probs, own_stats, stats, weights16,
    load_sem, piece_s, piece_r, z_s, z_r, ring_s, ring_r, core_s, core_r, halo_s, halo_r, stat_s, stat_r,
):
    th, tw = lax.axis_index("th"), lax.axis_index("tw")
    zh, y = th // 4, th % 4
    zl, x, core = tw // 8, (tw // 2) % 4, tw % 2
    z = zh * 2 + zl

    def at(zz, yy, xx, cc):
        return ((zz // 2) * 4 + yy, (zz % 2) * 8 + xx * 2 + cc)

    def tile(dr, dc):
        return ((th + dr + 16) % 16, (tw + dc + 16) % 16)

    north, south, west, east = tile(-1, 0), tile(1, 0), tile(0, -1), tile(0, 1)
    y_up, y_down = (y + 1) % 4, (y + 3) % 4
    x_up, x_down = (x + 1) % 4, (x + 3) % 4
    near_xc = [at(z, y, ((x * 2 + core + i) % 8) // 2, (core + i) % 2) for i in range(1, 8)]
    near_z = [at((z + i) % 8, y, x, core) for i in range(1, 8)]
    near_y = [at(z, y_up, x, core), at(z, y_down, x, core)]

    def remote(src, dst, send, recv, device):
        return pltpu.make_async_remote_copy(
            src_ref=src, dst_ref=dst, send_sem=send, recv_sem=recv,
            device_id=device, device_id_type=MESH,
        )

    barrier = pltpu.get_barrier_semaphore()
    greeted = [north, south, west, east] + near_xc + near_z + near_y
    for target in greeted:
        pl.semaphore_signal(barrier, inc=1, device_id=target, device_id_type=MESH)
    loads = []
    for number, (hbm, near) in enumerate(((k_hbm, kn), (v_hbm, vn), (q_hbm, qn))):
        for h in range(HEADS):
            loads.append(pltpu.make_async_copy(
                hbm.at[:, pl.ds(h * HD, HD)], near.at[h, OWN], load_sem.at[number, h]))
    loads.append(pltpu.make_async_copy(g_hbm, grads, load_sem.at[3, 0]))
    mine = x * 2 + core
    slab = core * 4 + x
    loads.append(pltpu.make_async_copy(w_hbm.at[slab], pieces.at[mine], load_sem.at[3, 1]))
    for copy in loads:
        copy.start()
    for copy in loads:
        copy.wait()
    pl.semaphore_wait(barrier, len(greeted))

    nears = (kn, vn, qn, dn)

    def halo(number, g, slot, source, device):
        near = nears[number]
        heads = pl.ds(g * PER, PER)
        return remote(near.at[heads, source], near.at[heads, slot],
                      halo_s.at[number, g, slot], halo_r.at[number, g, slot], device)

    def rows(number, g):
        halo(number, g, 3, OWN, south).start()
        halo(number, g, 5, OWN, north).start()

    def columns(number, g, dr):
        halo(number, g, 1 + dr, OWN + dr, east).start()
        halo(number, g, 7 + dr, OWN + dr, west).start()

    def arrived(number, g, slot):
        halo(number, g, slot, OWN, east).wait_recv()

    def rows_then_columns(number, g):
        arrived(number, g, 3)
        columns(number, g, -1)
        arrived(number, g, 5)
        columns(number, g, 1)

    def all_columns(number, g):
        for slot in (0, 1, 2, 6, 7, 8):
            arrived(number, g, slot)

    for i in range(1, 8):
        t = (mine + i) % 8
        remote(w_hbm.at[(t % 2) * 4 + t // 2], pieces.at[mine], piece_s.at[i - 1], piece_r.at[i - 1],
               near_xc[i - 1]).start()
    for number in (0, 1):
        for g in range(GROUPS):
            rows(number, g)
            columns(number, g, 0)
    for i in range(1, 8):
        remote(w_hbm.at[0], pieces.at[(mine + 8 - i) % 8], piece_s.at[i - 1], piece_r.at[i - 1],
               near_xc[i - 1]).wait_recv()
    block[...] = jnp.concatenate(
        [pieces[t].astype(F32)[0:6] for t in range(8)], axis=0).astype(BF)

    def z_place(zz):
        return wb.at[zz // 2, core, x, y, pl.ds((zz % 2) * 48, 48)]

    own_place = pltpu.make_async_copy(block, z_place(z), load_sem.at[3, 2])
    own_place.start()
    for i in range(1, 8):
        remote(block, z_place(z), z_s.at[i - 1], z_r.at[i - 1], near_z[i - 1]).start()
    own_place.wait()
    for i in range(1, 8):
        remote(block, z_place((z + 8 - i) % 8), z_s.at[i - 1], z_r.at[i - 1], near_z[i - 1]).wait_recv()

    y_dev = (at(z, y_up, x, core), at(z, y_down, x, core))
    x_dev = (at(z, y, x_up, core), at(z, y, x_down, core))
    other = at(z, y, x, 1 - core)
    half = lambda i: pl.ds(i * 2, 2)

    def ring(c, stage):
        along_y = (c % 2 == 0) == (stage == 0)
        if along_y:
            me, devs = y, y_dev
            if stage == 0:
                place = lambda p: wb.at[c, core, x, p]
                part = lambda p, i: wb.at[c, core, x, p, pl.ds(i * 48, 48)]
            else:
                place = lambda p: wb.at[c, core, :, p]
                part = lambda p, i: wb.at[c, core, half(i), p]
        else:
            me, devs = x, x_dev
            if stage == 0:
                place = lambda p: wb.at[c, core, p, y]
                part = lambda p, i: wb.at[c, core, p, y, pl.ds(i * 48, 48)]
            else:
                place = lambda p: wb.at[c, core, p]
                part = lambda p, i: wb.at[c, core, p, half(i)]
        return place, part, me, devs

    def ring_copy(c, stage, i, ref, device):
        return remote(ref, ref, ring_s.at[c, stage, i], ring_r.at[c, stage, i], device)

    def ring_start(c, stage):
        place, part, me, devs = ring(c, stage)
        ring_copy(c, stage, 0, place(me), devs[0]).start()
        ring_copy(c, stage, 1, place(me), devs[1]).start()

    def ring_relay(c, stage):
        place, part, me, devs = ring(c, stage)
        down, up = (me + 3) % 4, (me + 1) % 4
        ring_copy(c, stage, 0, place(down), devs[0]).wait_recv()
        ring_copy(c, stage, 2, part(down, 0), devs[0]).start()
        ring_copy(c, stage, 1, place(up), devs[1]).wait_recv()
        ring_copy(c, stage, 3, part(up, 1), devs[1]).start()
        return place(down), place(up)

    def ring_end(c, stage):
        place, part, me, devs = ring(c, stage)
        far = (me + 2) % 4
        ring_copy(c, stage, 2, part(far, 0), devs[0]).wait_recv()
        ring_copy(c, stage, 3, part(far, 1), devs[1]).wait_recv()
        return place(far)

    def core_copy(c, i):
        place, part, me, devs = ring(c, 1)
        ref = place((me + i) % 4)
        return remote(ref, ref, core_s.at[c, i], core_r.at[c, i], other)

    def core_arrival(c, i):
        along_y = c % 2 == 1
        p = ((y if along_y else x) + i) % 4
        ref = wb.at[c, 1 - core, :, p] if along_y else wb.at[c, 1 - core, p]
        return remote(ref, ref, core_s.at[c, i], core_r.at[c, i], other)

    for c in range(GROUPS):
        ring_start(c, 0)
    for c in range(GROUPS):
        ring_relay(c, 0)
    for c in range(GROUPS):
        ring_end(c, 0)
        ring_start(c, 1)
        core_copy(c, 0).start()
    for c in range(GROUPS):
        ring_relay(c, 1)
        core_copy(c, 1).start()
        core_copy(c, 3).start()
    for g in range(GROUPS):
        rows_then_columns(0, g)
        rows_then_columns(1, g)
    for g in range(GROUPS):
        rows(2, g)
        columns(2, g, 0)
    for c in range(GROUPS):
        ring_end(c, 1)
        core_copy(c, 2).start()
        for i in range(4):
            core_arrival(c, i).wait_recv()
        total = jnp.zeros((TOK, PER * HD), F32)
        for s in range(SLABS):
            w = wb[c, s // 4, s % 4].reshape(PER * HD, SLABW)
            total += nt(grads[:, s * SLABW:(s + 1) * SLABW], w)
        for i in range(PER):
            dn[c * PER + i, OWN] = total[:, i * HD:(i + 1) * HD].astype(BF)
        rows(3, c)
        columns(3, c, 0)

    lane = lax.broadcasted_iota(jnp.int32, (1, CELLS), 1)
    slot, token = lane // TOK, lane % TOK
    dr, dc = slot % 3 - 1, slot // 3 - 1
    row = (th + dr) * 8 + (token // 8) % 8
    col = (tw + dc) * 8 + token % 8
    limit_rows, limit_cols = 128 - pad_ref[0], 128 - pad_ref[1]
    key_ok = (row >= 0) & (row < limit_rows) & (col >= 0) & (col < limit_cols)
    query_ok = (row >= 0) & (row < 128) & (col >= 0) & (col < 128)
    key_bias = jnp.where(key_ok, 0.0, MASKED)
    query_bias = jnp.where(query_ok, 0.0, MASKED)
    far_rows, far_cols = jnp.abs(dr), jnp.abs(dc)

    def window(h, bias):
        inside = (far_rows <= ext_ref[0, h]) & (far_cols <= ext_ref[1, h])
        return jnp.where(inside, bias, MASKED)

    lane_of = lax.broadcasted_iota(jnp.int32, (TOK, TOK), 1)
    for g in range(GROUPS):
        all_columns(0, g)
        all_columns(1, g)

    def forward(g, found):
        for i in range(PER):
            h = g * PER + i
            s = nt(qn[h, OWN], kn[h].reshape(CELLS, HD)) * FACTOR + window(h, key_bias)
            top = jnp.max(s, axis=1, keepdims=True)
            p = jnp.exp(s - top)
            summed = jnp.sum(p, axis=1, keepdims=True)
            w = (p * (1.0 / summed)).astype(BF)
            probs[h] = w
            o = nn(w, vn[h].reshape(CELLS, HD)).astype(BF)
            att[g, :, i * HD:(i + 1) * HD] = o
            correction = jnp.sum(o.astype(F32) * dn[h, OWN].astype(F32), axis=1, keepdims=True)
            found = jnp.where(lane_of == h, top + jnp.log(summed), found)
            found = jnp.where(lane_of == HEADS + h, correction, found)
        return found

    found = lax.fori_loop(0, GROUPS, forward, jnp.zeros((TOK, TOK), F32))
    own_stats[...] = found
    stats[OWN] = found.T

    def stat(slot, source, device):
        return remote(stats.at[source], stats.at[slot], stat_s.at[slot], stat_r.at[slot], device)

    stat(3, OWN, south).start()
    stat(5, OWN, north).start()
    stat(1, OWN, east).start()
    stat(7, OWN, west).start()

    for g in range(GROUPS):
        rows_then_columns(2, g)
        rows_then_columns(3, g)

    for s in range(SLABS):
        total = jnp.zeros((TOK, SLABW), F32)
        for c in range(GROUPS):
            total += nn(att[c], wb[c, s // 4, s % 4].reshape(PER * HD, SLABW))
        out_ref[:, s * SLABW:(s + 1) * SLABW] = total.astype(BF)

    stat(3, OWN, south).wait_recv()
    stat(0, 3, east).start()
    stat(6, 3, west).start()
    stat(5, OWN, north).wait_recv()
    stat(2, 5, east).start()
    stat(8, 5, west).start()

    def query_part(g, carry):
        for i in range(PER):
            h = g * PER + i
            correction = jnp.sum(jnp.where(lane_of == HEADS + h, own_stats[...], 0.0), axis=1, keepdims=True)
            dp = nt(dn[h, OWN], vn[h].reshape(CELLS, HD))
            ds = (probs[h].astype(F32) * (dp - correction)).astype(BF)
            dq = nn(ds, kn[h].reshape(CELLS, HD)) * FACTOR
            dq_ref[:, pl.ds(pl.multiple_of(h * HD, HD), HD)] = dq.astype(BF)
        return carry

    lax.fori_loop(0, GROUPS, query_part, 0)

    for slot in (0, 1, 2, 6, 7, 8):
        stat(slot, OWN, east).wait_recv()
    for g in range(GROUPS):
        all_columns(2, g)
        all_columns(3, g)
    cell = lax.broadcasted_iota(jnp.int32, (TOK, 1), 0)
    own_ok = (th * 8 + (cell // 8) % 8 < limit_rows) & (tw * 8 + cell % 8 < limit_cols)

    def key_part(g, carry):
        for i in range(PER):
            h = g * PER + i
            totals = jnp.concatenate([stats[j, pl.ds(h, 1)] for j in range(9)], axis=1)
            corrections = jnp.concatenate([stats[j, pl.ds(HEADS + h, 1)] for j in range(9)], axis=1)
            shift = window(h, query_bias) - totals
            qs = qn[h].reshape(CELLS, HD)
            ds_near = dn[h].reshape(CELLS, HD)
            w = jnp.exp(nt(kn[h, OWN], qs) * FACTOR + shift)
            dp = nt(vn[h, OWN], ds_near)
            ds = (w * (dp - corrections)).astype(BF)
            dk = jnp.where(own_ok, nn(ds, qs) * FACTOR, 0.0)
            dv = jnp.where(own_ok, nn(w.astype(BF), ds_near), 0.0)
            at_h = pl.ds(pl.multiple_of(h * HD, HD), HD)
            dk_ref[:, at_h] = dk.astype(BF)
            dv_ref[:, at_h] = dv.astype(BF)
        return carry

    lax.fori_loop(0, GROUPS, key_part, 0)

    for i in range(1, 8):
        remote(w_hbm.at[0], pieces.at[0], piece_s.at[i - 1], piece_r.at[i - 1], near_xc[i - 1]).wait_send()
        remote(block, z_place(z), z_s.at[i - 1], z_r.at[i - 1], near_z[i - 1]).wait_send()
    for c in range(GROUPS):
        for stage in range(2):
            place, part, me, devs = ring(c, stage)
            for i in range(2):
                ring_copy(c, stage, i, place(me), devs[i]).wait_send()
                ring_copy(c, stage, 2 + i, part(me, 0), devs[i]).wait_send()
        for i in range(4):
            core_copy(c, i).wait_send()
    for number in range(4):
        for g in range(GROUPS):
            for slot in (0, 1, 2, 3, 5, 6, 7, 8):
                halo(number, g, slot, OWN, east).wait_send()
    for slot in (0, 1, 2, 3, 5, 6, 7, 8):
        stat(slot, OWN, east).wait_send()


def on_device(q, k, v, out_grad, out_weight, extent, pad):
    shape = q.shape
    flat = lambda a: a.reshape(TOK, a.shape[-1])
    pieces = out_weight.reshape(6, SLABS, SLABW).transpose(1, 0, 2)
    pieces = jnp.pad(pieces, ((0, 0), (0, 10), (0, 0)))
    hbm = pl.BlockSpec(memory_space=pl.ANY)
    smem = pl.BlockSpec(memory_space=pltpu.SMEM)
    vmem = pl.BlockSpec(memory_space=pltpu.VMEM)
    near = pltpu.VMEM((HEADS, 9, TOK, HD), BF)
    dma = pltpu.SemaphoreType.DMA
    out, dq, dk, dv = pl.pallas_call(
        kernel,
        out_shape=(
            jax.ShapeDtypeStruct((TOK, D), BF),
            jax.ShapeDtypeStruct((TOK, E), BF),
            jax.ShapeDtypeStruct((TOK, E), BF),
            jax.ShapeDtypeStruct((TOK, E), BF),
        ),
        in_specs=[smem, smem, hbm, hbm, hbm, hbm, vmem],
        out_specs=(vmem, vmem, vmem, vmem),
        scratch_shapes=[
            near, near, near, near,
            pltpu.VMEM((GROUPS, 2, 4, 4, 96, SLABW), BF),
            pltpu.VMEM((TOK, D), BF),
            pltpu.VMEM((8, 16, SLABW), BF),
            pltpu.VMEM((48, SLABW), BF),
            pltpu.VMEM((GROUPS, TOK, PER * HD), BF),
            pltpu.VMEM((HEADS, TOK, CELLS), BF),
            pltpu.VMEM((TOK, TOK), F32),
            pltpu.VMEM((9, TOK, TOK), F32),
            pltpu.VMEM((16, 128), BF),
            dma((4, HEADS)),
            dma((7,)), dma((7,)), dma((7,)), dma((7,)),
            dma((GROUPS, 2, 4)), dma((GROUPS, 2, 4)),
            dma((GROUPS, 4)), dma((GROUPS, 4)),
            dma((4, GROUPS, 9)), dma((4, GROUPS, 9)),
            dma((9,)), dma((9,)),
        ],
        compiler_params=pltpu.CompilerParams(
            collective_id=0, has_side_effects=True, vmem_limit_bytes=60 * 1024 * 1024),
        cost_estimate=pl.CostEstimate(flops=7 * 10**9, bytes_accessed=6 * 10**6, transcendentals=4 * 10**6),
    )(extent, pad, flat(q), flat(k), flat(v), flat(out_grad), pieces)
    return (out.reshape(out_grad.shape), dq.reshape(shape), dk.reshape(shape), dv.reshape(shape))


def solution(mesh):
    cells = P(None, "th", "tw", None)
    return jax.shard_map(
        on_device,
        mesh=mesh,
        in_specs=(cells, cells, cells, cells, P(("th", "tw"), None), P(), P()),
        out_specs=(cells, cells, cells, cells),
        check_vma=False,
    )
```

time: 583 us -> 190 us (0.33)
  the two profiles are of different devices: /device:TPU:1 before, /device:TPU:63 now
where the time goes in v1:
time: 190 us
  Pallas kernels  182 us (96%)
  local copies, waits for them, and re-layouts  6.59 us (3%)
    pallas_call x1, Pallas kernels, on_device(): pl.pallas_call(kernel, out_shape=(jax.ShapeDtypeStruct((TOK, D), BF), jax...  182 us
    unnamed x10, local copies, waits for them, and re-layouts  5.14 us

profile of v1, /device:TPU:63, one launch (start us, length us, event | category | flops | bytes accessed | tf_op | source)
XLA Modules:
  0.0 189.6 jit_solution(11862067490034338009)
XLA Ops:
  0.6 1.5 pad.4.w_hbm
  2.1 182.4 %shard_map.102 = (bf16[128,3072]{1,0:T(8,128)(2,1)}, bf16[128,1536]{1,0:T(8,128)(2,1)}, bf16[128,1536]{1,0:T(8,128)(2,1)}, bf16[128,1536]{1,0:T(8,128)(2,1)}) custom-call(s32[2,12]{1,0:T(2,128)} %ext_ref.1, s32[2]{0:T(128)} %pad_ref.1, bf16[128,1536]{1,0:T(8,128)(2,1)} %bitcast.17, bf16[128,1536]{1,0:T(8,128)(2,1)} %bitcast.18, bf16[128,1536]{1,0:T(8,128)(2,1)} %bitcast.19, ...), custom_call_target="tpu_custom_call" | custom-call | flops 7000000000 | bytes 6000000 | tf_op jit(solution)/shard_map/pallas_call | solution.py:359
  184.5 0.0 copy-start.2
  184.5 2.1 %copy.15 = bf16[2,8,8,3072]{3,2,1,0:T(8,128)(2,1)} copy(bf16[2,8,8,3072]{3,2,1,0:T(8,128)(2,1)} %bitcast.11) | data formatting | bytes 1572864
  186.6 0.0 copy-done.2
  186.6 0.0 copy-start.1
  186.6 0.7 copy.16
  187.4 0.4 copy-done.1
  187.8 0.0 copy-start
  187.8 0.7 copy.17
  188.5 0.4 copy-done
  188.9 0.7 copy.18
Async XLA Ops:
  184.5 2.1 %copy-start.2 = (bf16[128,1536]{1,0:T(8,128)(2,1)S(1)}, bf16[128,1536]{1,0:T(8,128)(2,1)}, u32[]{:S(2)}) copy-start(bf16[128,1536]{1,0:T(8,128)(2,1)} %get-tuple-element.9) | copy-start | bytes 1179652
  186.6 1.1 copy-start.1
  187.8 1.1 copy-start

commit v2 on v1

--- a/solution.py
+++ b/solution.py
@@ -12,6 +12,9 @@
 SLABS = 8
 SLABW = D // SLABS
 OWN = 4
+RELAYED = (2, 3)
+ORDER = (2, 3, 0, 1)
+Y_FIRST = (1, 3)
 CELLS = 9 * TOK
 MASKED = -1e30
 FACTOR = HD ** (-0.5)
@@ -31,6 +34,7 @@
     out_ref, dq_ref, dk_ref, dv_ref,
     qn, kn, vn, dn, wb, grads, pieces, block, att, probs, own_stats, stats, weights16,
     load_sem, piece_s, piece_r, z_s, z_r, ring_s, ring_r, core_s, core_r, halo_s, halo_r, stat_s, stat_r,
+    row_relay, col_relay, row_rs, row_rr, col_rs, col_rr,
 ):
     th, tw = lax.axis_index("th"), lax.axis_index("tw")
     zh, y = th // 4, th % 4
@@ -71,6 +75,12 @@
     loads.append(pltpu.make_async_copy(w_hbm.at[slab], pieces.at[mine], load_sem.at[3, 1]))
     for copy in loads:
         copy.start()
+    for edge, slots in ((tw == 0, (0, 1, 2)), (tw == 15, (6, 7, 8))):
+        @pl.when(edge)
+        def _():
+            for near in (kn, vn, qn, dn):
+                for j in slots:
+                    near[:, j] = jnp.zeros((HEADS, TOK, HD), BF)
     for copy in loads:
         copy.wait()
     pl.semaphore_wait(barrier, len(greeted))
@@ -83,16 +93,85 @@
         return remote(near.at[heads, source], near.at[heads, slot],
                       halo_s.at[number, g, slot], halo_r.at[number, g, slot], device)
 
+    first_row, last_row = y == 0, y == 3
+    first_col, last_col = tw == 0, tw == 15
+    cross_east, cross_west = tw == 7, tw == 8
+
+    def via(number, g, slot, source, space, send, recv, device):
+        return remote(nears[number].at[pl.ds(g * PER, PER), source], space, send, recv, device)
+
     def rows(number, g):
-        halo(number, g, 3, OWN, south).start()
-        halo(number, g, 5, OWN, north).start()
+        if g in RELAYED:
+            i = g - RELAYED[0]
+            for slot, crossing, straight, device in (
+                (3, last_row, south, tile(-3, 0)), (5, first_row, north, tile(3, 0))):
+                @pl.when(crossing)
+                def _():
+                    via(number, g, slot, OWN, row_relay.at[number, i], halo_s.at[number, g, slot],
+                        row_rr.at[number, i], device).start()
+
+                @pl.when(jnp.logical_not(crossing))
+                def _():
+                    halo(number, g, slot, OWN, straight).start()
+        else:
+            halo(number, g, 3, OWN, south).start()
+            halo(number, g, 5, OWN, north).start()
+
+    def row_pass(number, g, slot, device):
+        i = g - RELAYED[0]
+        return remote(row_relay.at[number, i], nears[number].at[pl.ds(g * PER, PER), slot],
+                      row_rs.at[number, i], halo_r.at[number, g, slot], device)
+
+    def pass_rows(number, g):
+        if g not in RELAYED:
+            return
+        i = g - RELAYED[0]
+        for slot, crossing, device in ((3, first_row, tile(4, 0)), (5, last_row, tile(-4, 0))):
+            @pl.when(crossing)
+            def _():
+                via(number, g, slot, OWN, row_relay.at[number, i], row_rs.at[number, i],
+                    row_rr.at[number, i], north).wait_recv()
+                row_pass(number, g, slot, device).start()
 
     def columns(number, g, dr):
-        halo(number, g, 1 + dr, OWN + dr, east).start()
-        halo(number, g, 7 + dr, OWN + dr, west).start()
+        for slot, crossing, edge, straight, device in (
+            (1 + dr, cross_east, last_col, east, tile(0, -7)),
+            (7 + dr, cross_west, first_col, west, tile(0, 7))):
+            if g in RELAYED:
+                i = g - RELAYED[0]
+
+                @pl.when(crossing)
+                def _():
+                    via(number, g, slot, OWN + dr, col_relay.at[number, i, dr + 1],
+                        halo_s.at[number, g, slot], col_rr.at[number, i, dr + 1], device).start()
+
+                @pl.when(jnp.logical_not(crossing | edge))
+                def _():
+                    halo(number, g, slot, OWN + dr, straight).start()
+            else:
+                @pl.when(jnp.logical_not(edge))
+                def _():
+                    halo(number, g, slot, OWN + dr, straight).start()
+
+    def col_pass(number, g, dr, slot, device):
+        i = g - RELAYED[0]
+        return remote(col_relay.at[number, i, dr + 1], nears[number].at[pl.ds(g * PER, PER), slot],
+                      col_rs.at[number, i, dr + 1], halo_r.at[number, g, slot], device)
+
+    def pass_columns(number, g, drs=(0, -1, 1)):
+        if g not in RELAYED:
+            return
+        i = g - RELAYED[0]
+        for base, edge, device in ((1, first_col, tile(0, 8)), (7, last_col, tile(0, -8))):
+            @pl.when(edge)
+            def _():
+                for dr in drs:
+                    via(number, g, OWN, OWN, col_relay.at[number, i, dr + 1], col_rs.at[number, i, dr + 1],
+                        col_rr.at[number, i, dr + 1], north).wait_recv()
+                    col_pass(number, g, dr, base + dr, device).start()
 
     def arrived(number, g, slot):
-        halo(number, g, slot, OWN, east).wait_recv()
+        halo(number, g, slot, OWN, north).wait_recv()
 
     def rows_then_columns(number, g):
         arrived(number, g, 3)
@@ -101,15 +180,22 @@
         columns(number, g, 1)
 
     def all_columns(number, g):
-        for slot in (0, 1, 2, 6, 7, 8):
-            arrived(number, g, slot)
+        @pl.when(jnp.logical_not(first_col))
+        def _():
+            for slot in (0, 1, 2):
+                arrived(number, g, slot)
+
+        @pl.when(jnp.logical_not(last_col))
+        def _():
+            for slot in (6, 7, 8):
+                arrived(number, g, slot)
 
     for i in range(1, 8):
         t = (mine + i) % 8
         remote(w_hbm.at[(t % 2) * 4 + t // 2], pieces.at[mine], piece_s.at[i - 1], piece_r.at[i - 1],
                near_xc[i - 1]).start()
     for number in (0, 1):
-        for g in range(GROUPS):
+        for g in ORDER:
             rows(number, g)
             columns(number, g, 0)
     for i in range(1, 8):
@@ -126,6 +212,10 @@
     for i in range(1, 8):
         remote(block, z_place(z), z_s.at[i - 1], z_r.at[i - 1], near_z[i - 1]).start()
     own_place.wait()
+    for number in (0, 1):
+        for g in RELAYED:
+            pass_rows(number, g)
+            pass_columns(number, g, (0,))
     for i in range(1, 8):
         remote(block, z_place((z + 8 - i) % 8), z_s.at[i - 1], z_r.at[i - 1], near_z[i - 1]).wait_recv()
 
@@ -135,7 +225,7 @@
     half = lambda i: pl.ds(i * 2, 2)
 
     def ring(c, stage):
-        along_y = (c % 2 == 0) == (stage == 0)
+        along_y = (c in Y_FIRST) == (stage == 0)
         if along_y:
             me, devs = y, y_dev
             if stage == 0:
@@ -184,29 +274,31 @@
         return remote(ref, ref, core_s.at[c, i], core_r.at[c, i], other)
 
     def core_arrival(c, i):
-        along_y = c % 2 == 1
+        along_y = c not in Y_FIRST
         p = ((y if along_y else x) + i) % 4
         ref = wb.at[c, 1 - core, :, p] if along_y else wb.at[c, 1 - core, p]
         return remote(ref, ref, core_s.at[c, i], core_r.at[c, i], other)
 
     for c in range(GROUPS):
         ring_start(c, 0)
+    for g in ORDER:
+        rows(2, g)
+        columns(2, g, 0)
     for c in range(GROUPS):
         ring_relay(c, 0)
     for c in range(GROUPS):
         ring_end(c, 0)
         ring_start(c, 1)
         core_copy(c, 0).start()
+    for g in RELAYED:
+        pass_rows(2, g)
+        pass_columns(2, g, (0,))
     for c in range(GROUPS):
+        rows_then_columns(0, c)
+        rows_then_columns(1, c)
         ring_relay(c, 1)
         core_copy(c, 1).start()
         core_copy(c, 3).start()
-    for g in range(GROUPS):
-        rows_then_columns(0, g)
-        rows_then_columns(1, g)
-    for g in range(GROUPS):
-        rows(2, g)
-        columns(2, g, 0)
     for c in range(GROUPS):
         ring_end(c, 1)
         core_copy(c, 2).start()
@@ -220,6 +312,9 @@
             dn[c * PER + i, OWN] = total[:, i * HD:(i + 1) * HD].astype(BF)
         rows(3, c)
         columns(3, c, 0)
+        pass_columns(0, c, (-1, 1))
+        pass_columns(1, c, (-1, 1))
+        rows_then_columns(2, c)
 
     lane = lax.broadcasted_iota(jnp.int32, (1, CELLS), 1)
     slot, token = lane // TOK, lane % TOK
@@ -238,11 +333,10 @@
         return jnp.where(inside, bias, MASKED)
 
     lane_of = lax.broadcasted_iota(jnp.int32, (TOK, TOK), 1)
-    for g in range(GROUPS):
+
+    def forward(g, found):
         all_columns(0, g)
         all_columns(1, g)
-
-    def forward(g, found):
         for i in range(PER):
             h = g * PER + i
             s = nt(qn[h, OWN], kn[h].reshape(CELLS, HD)) * FACTOR + window(h, key_bias)
@@ -270,8 +364,11 @@
     stat(1, OWN, east).start()
     stat(7, OWN, west).start()
 
+    for g in RELAYED:
+        pass_rows(3, g)
+        pass_columns(3, g, (0,))
+        pass_columns(2, g, (-1, 1))
     for g in range(GROUPS):
-        rows_then_columns(2, g)
         rows_then_columns(3, g)
 
     for s in range(SLABS):
@@ -299,15 +396,16 @@
 
     lax.fori_loop(0, GROUPS, query_part, 0)
 
+    for g in range(GROUPS):
+        pass_columns(3, g, (-1, 1))
     for slot in (0, 1, 2, 6, 7, 8):
         stat(slot, OWN, east).wait_recv()
-    for g in range(GROUPS):
+    cell = lax.broadcasted_iota(jnp.int32, (TOK, 1), 0)
+    own_ok = (th * 8 + (cell // 8) % 8 < limit_rows) & (tw * 8 + cell % 8 < limit_cols)
+
+    def key_part(g, carry):
         all_columns(2, g)
         all_columns(3, g)
-    cell = lax.broadcasted_iota(jnp.int32, (TOK, 1), 0)
-    own_ok = (th * 8 + (cell // 8) % 8 < limit_rows) & (tw * 8 + cell % 8 < limit_cols)
-
-    def key_part(g, carry):
         for i in range(PER):
             h = g * PER + i
             totals = jnp.concatenate([stats[j, pl.ds(h, 1)] for j in range(9)], axis=1)
@@ -340,8 +438,22 @@
             core_copy(c, i).wait_send()
     for number in range(4):
         for g in range(GROUPS):
-            for slot in (0, 1, 2, 3, 5, 6, 7, 8):
-                halo(number, g, slot, OWN, east).wait_send()
+            halo(number, g, 3, OWN, north).wait_send()
+            halo(number, g, 5, OWN, north).wait_send()
+            for edge, slots in ((last_col, (0, 1, 2)), (first_col, (6, 7, 8))):
+                @pl.when(jnp.logical_not(edge))
+                def _():
+                    for slot in slots:
+                        halo(number, g, slot, OWN, north).wait_send()
+            if g in RELAYED:
+                @pl.when(first_row | last_row)
+                def _():
+                    row_pass(number, g, 3, north).wait_send()
+
+                @pl.when(first_col | last_col)
+                def _():
+                    for dr in (-1, 0, 1):
+                        col_pass(number, g, dr, OWN, north).wait_send()
     for slot in (0, 1, 2, 3, 5, 6, 7, 8):
         stat(slot, OWN, east).wait_send()
 
@@ -383,6 +495,9 @@
             dma((GROUPS, 4)), dma((GROUPS, 4)),
             dma((4, GROUPS, 9)), dma((4, GROUPS, 9)),
             dma((9,)), dma((9,)),
+            pltpu.VMEM((4, 2, PER, TOK, HD), BF),
+            pltpu.VMEM((4, 2, 3, PER, TOK, HD), BF),
+            dma((4, 2)), dma((4, 2)), dma((4, 2, 3)), dma((4, 2, 3)),
         ],
         compiler_params=pltpu.CompilerParams(
             collective_id=0, has_side_effects=True, vmem_limit_bytes=60 * 1024 * 1024),

time: 190 us -> 137 us (0.72)
  the two profiles are of different devices: /device:TPU:63 before, /device:TPU:32 now
where the time goes in v2:
time: 137 us
  Pallas kernels  129 us (94%)
  local copies, waits for them, and re-layouts  6.59 us (5%)
    pallas_call x1, Pallas kernels, on_device(): pl.pallas_call(kernel, out_shape=(jax.ShapeDtypeStruct((TOK, D), BF), jax...  129 us
    unnamed x10, local copies, waits for them, and re-layouts  5.14 us

profile of v2, /device:TPU:32, one launch (start us, length us, event | category | flops | bytes accessed | tf_op | source)
XLA Modules:
  0.0 136.6 jit_solution(15838037369073307102)
XLA Ops:
  0.6 1.5 %pad.4.w_hbm = bf16[8,16,384]{2,1,0:T(8,128)(2,1)} pad(bf16[8,6,384]{2,1,0:T(8,128)(2,1)} %bitcast.15, bf16[]{:T(256)} %constant.2.clone.1), padding=0_0x0_10x0_0 | pad | bytes 135170 | tf_op jit(solution)/shard_map/jit(_pad)/pad | solution.py:465
  2.1 129.4 %shard_map.102 = (bf16[128,3072]{1,0:T(8,128)(2,1)}, bf16[128,1536]{1,0:T(8,128)(2,1)}, bf16[128,1536]{1,0:T(8,128)(2,1)}, bf16[128,1536]{1,0:T(8,128)(2,1)}) custom-call(s32[2,12]{1,0:T(2,128)} %ext_ref.1, s32[2]{0:T(128)} %pad_ref.1, bf16[128,1536]{1,0:T(8,128)(2,1)} %bitcast.17, bf16[128,1536]{1,0:T(8,128)(2,1)} %bitcast.18, bf16[128,1536]{1,0:T(8,128)(2,1)} %bitcast.19, ...), custom_call_target="tpu_custom_call" | custom-call | flops 7000000000 | bytes 6000000 | tf_op jit(solution)/shard_map/pallas_call | solution.py:471
  131.5 0.0 copy-start.2
  131.5 2.1 %copy.15 = bf16[2,8,8,3072]{3,2,1,0:T(8,128)(2,1)} copy(bf16[2,8,8,3072]{3,2,1,0:T(8,128)(2,1)} %bitcast.11) | data formatting | bytes 1572864
  133.6 0.0 copy-done.2
  133.6 0.0 copy-start.1
  133.6 0.7 copy.16
  134.4 0.4 copy-done.1
  134.8 0.0 copy-start
  134.8 0.7 copy.17
  135.5 0.4 copy-done
  135.9 0.7 copy.18
Async XLA Ops:
  131.5 2.1 %copy-start.2 = (bf16[128,1536]{1,0:T(8,128)(2,1)S(1)}, bf16[128,1536]{1,0:T(8,128)(2,1)}, u32[]{:S(2)}) copy-start(bf16[128,1536]{1,0:T(8,128)(2,1)} %get-tuple-element.9) | copy-start | bytes 1179652
  133.6 1.1 copy-start.1
  134.8 1.1 copy-start

commit v3 on v2

--- a/solution.py
+++ b/solution.py
@@ -1,3 +1,5 @@
+import functools
+
 import jax
 import jax.numpy as jnp
 from jax import lax
@@ -16,6 +18,7 @@
 ORDER = (2, 3, 0, 1)
 Y_FIRST = (1, 3)
 CELLS = 9 * TOK
+SIZES = ((9, 7, 4), (9, 9, 6), (12, 12, 12))
 MASKED = -1e30
 FACTOR = HD ** (-0.5)
 BF, F32 = jnp.bfloat16, jnp.float32
@@ -30,11 +33,11 @@
 
 
 def kernel(
-    ext_ref, pad_ref, q_hbm, k_hbm, v_hbm, g_hbm, w_hbm,
+    sizes, ext_ref, pad_ref, q_hbm, k_hbm, v_hbm, g_hbm, w_ref,
     out_ref, dq_ref, dk_ref, dv_ref,
-    qn, kn, vn, dn, wb, grads, pieces, block, att, probs, own_stats, stats, weights16,
+    qn, kn, vn, dn, wb, grads, pieces, block, att, probs, own_stats, stats,
     load_sem, piece_s, piece_r, z_s, z_r, ring_s, ring_r, core_s, core_r, halo_s, halo_r, stat_s, stat_r,
-    row_relay, col_relay, row_rs, row_rr, col_rs, col_rr,
+    row_relay, col_relay, natural, place_ref, padded, row_rs, row_rr, col_rs, col_rr,
 ):
     th, tw = lax.axis_index("th"), lax.axis_index("tw")
     zh, y = th // 4, th % 4
@@ -65,16 +68,55 @@
     for target in greeted:
         pl.semaphore_signal(barrier, inc=1, device_id=target, device_id_type=MESH)
     loads = []
-    for number, (hbm, near) in enumerate(((k_hbm, kn), (v_hbm, vn), (q_hbm, qn))):
+    for number, hbm in enumerate((k_hbm, v_hbm, q_hbm)):
         for h in range(HEADS):
             loads.append(pltpu.make_async_copy(
-                hbm.at[:, pl.ds(h * HD, HD)], near.at[h, OWN], load_sem.at[number, h]))
+                hbm.at[:, pl.ds(h * HD, HD)], natural.at[number, h], load_sem.at[number, h]))
     loads.append(pltpu.make_async_copy(g_hbm, grads, load_sem.at[3, 0]))
     mine = x * 2 + core
     slab = core * 4 + x
-    loads.append(pltpu.make_async_copy(w_hbm.at[slab], pieces.at[mine], load_sem.at[3, 1]))
     for copy in loads:
         copy.start()
+    padded[...] = jnp.zeros_like(padded)
+    padded[:, 0:6, :] = w_ref[...]
+    own_piece = pltpu.make_async_copy(padded.at[slab], pieces.at[mine], load_sem.at[3, 1])
+    own_piece.start()
+
+    n_rows, n_cols, n_both = sizes
+    row_only, col_only = n_rows - n_both, n_cols - n_both
+    none_left = HEADS - n_rows - col_only
+    in_rows = [ext_ref[0, h] for h in range(HEADS)]
+    in_cols = [ext_ref[1, h] for h in range(HEADS)]
+    used = [jnp.int32(0)] * 4
+    places = [jnp.int32(0)] * HEADS
+    starts = (0, row_only, n_rows, n_rows + col_only)
+    room = (row_only, n_both, col_only, none_left)
+    for wanted_rows, wanted_cols, pools in ((1, 1, (1,)), (1, 0, (0, 1)), (0, 1, (2, 1)), (0, 0, (3, 0, 2, 1))):
+        for h in range(HEADS):
+            open_now = (in_rows[h] == wanted_rows) & (in_cols[h] == wanted_cols)
+            for pool in pools:
+                take = open_now if pool == pools[-1] else open_now & (used[pool] < room[pool])
+                places[h] = jnp.where(take, starts[pool] + used[pool], places[h])
+                used[pool] = used[pool] + take.astype(jnp.int32)
+                open_now = open_now & jnp.logical_not(take)
+    for h in range(HEADS):
+        place_ref[h] = places[h]
+    heads_at = [
+        sum(jnp.where(places[h] == p, h, 0) for h in range(HEADS)) for p in range(HEADS)]
+
+    ranges = {}
+    for j in (3, 5):
+        ranges[j] = (0, n_rows)
+    for j in (1, 7):
+        ranges[j] = (row_only, n_rows + col_only)
+    for j in (0, 2, 6, 8):
+        ranges[j] = (row_only, n_rows)
+    for near in (kn, vn, qn):
+        for j, (low, high) in ranges.items():
+            if low:
+                near[0:low, j] = jnp.zeros((low, TOK, HD), BF)
+            if high < HEADS:
+                near[high:HEADS, j] = jnp.zeros((HEADS - high, TOK, HD), BF)
     for edge, slots in ((tw == 0, (0, 1, 2)), (tw == 15, (6, 7, 8))):
         @pl.when(edge)
         def _():
@@ -83,13 +125,24 @@
                     near[:, j] = jnp.zeros((HEADS, TOK, HD), BF)
     for copy in loads:
         copy.wait()
+    own_piece.wait()
+    for p in range(HEADS):
+        for number, near in enumerate((kn, vn, qn)):
+            near[p, OWN] = natural[number, heads_at[p]]
     pl.semaphore_wait(barrier, len(greeted))
 
     nears = (kn, vn, qn, dn)
+
+    def span(number, g, slot):
+        if number == 3:
+            return g * PER, PER
+        low, high = ranges[slot]
+        first = low + (high - low) * g // GROUPS
+        return first, low + (high - low) * (g + 1) // GROUPS - first
 
     def halo(number, g, slot, source, device):
         near = nears[number]
-        heads = pl.ds(g * PER, PER)
+        heads = pl.ds(*span(number, g, slot))
         return remote(near.at[heads, source], near.at[heads, slot],
                       halo_s.at[number, g, slot], halo_r.at[number, g, slot], device)
 
@@ -98,7 +151,8 @@
     cross_east, cross_west = tw == 7, tw == 8
 
     def via(number, g, slot, source, space, send, recv, device):
-        return remote(nears[number].at[pl.ds(g * PER, PER), source], space, send, recv, device)
+        first, count = span(number, g, slot)
+        return remote(nears[number].at[pl.ds(first, count), source], space.at[pl.ds(0, count)], send, recv, device)
 
     def rows(number, g):
         if g in RELAYED:
@@ -119,7 +173,8 @@
 
     def row_pass(number, g, slot, device):
         i = g - RELAYED[0]
-        return remote(row_relay.at[number, i], nears[number].at[pl.ds(g * PER, PER), slot],
+        first, count = span(number, g, slot)
+        return remote(row_relay.at[number, i, pl.ds(0, count)], nears[number].at[pl.ds(first, count), slot],
                       row_rs.at[number, i], halo_r.at[number, g, slot], device)
 
     def pass_rows(number, g):
@@ -155,7 +210,8 @@
 
     def col_pass(number, g, dr, slot, device):
         i = g - RELAYED[0]
-        return remote(col_relay.at[number, i, dr + 1], nears[number].at[pl.ds(g * PER, PER), slot],
+        first, count = span(number, g, slot)
+        return remote(col_relay.at[number, i, dr + 1, pl.ds(0, count)], nears[number].at[pl.ds(first, count), slot],
                       col_rs.at[number, i, dr + 1], halo_r.at[number, g, slot], device)
 
     def pass_columns(number, g, drs=(0, -1, 1)):
@@ -166,7 +222,7 @@
             @pl.when(edge)
             def _():
                 for dr in drs:
-                    via(number, g, OWN, OWN, col_relay.at[number, i, dr + 1], col_rs.at[number, i, dr + 1],
+                    via(number, g, base + dr, OWN, col_relay.at[number, i, dr + 1], col_rs.at[number, i, dr + 1],
                         col_rr.at[number, i, dr + 1], north).wait_recv()
                     col_pass(number, g, dr, base + dr, device).start()
 
@@ -179,6 +235,14 @@
         arrived(number, g, 5)
         columns(number, g, 1)
 
+    def all_rows_then_columns(number):
+        for g in range(GROUPS):
+            arrived(number, g, 3)
+            arrived(number, g, 5)
+        for g in ORDER:
+            columns(number, g, -1)
+            columns(number, g, 1)
+
     def all_columns(number, g):
         @pl.when(jnp.logical_not(first_col))
         def _():
@@ -192,14 +256,14 @@
 
     for i in range(1, 8):
         t = (mine + i) % 8
-        remote(w_hbm.at[(t % 2) * 4 + t // 2], pieces.at[mine], piece_s.at[i - 1], piece_r.at[i - 1],
+        remote(padded.at[(t % 2) * 4 + t // 2], pieces.at[mine], piece_s.at[i - 1], piece_r.at[i - 1],
                near_xc[i - 1]).start()
     for number in (0, 1):
         for g in ORDER:
             rows(number, g)
             columns(number, g, 0)
     for i in range(1, 8):
-        remote(w_hbm.at[0], pieces.at[(mine + 8 - i) % 8], piece_s.at[i - 1], piece_r.at[i - 1],
+        remote(padded.at[0], pieces.at[(mine + 8 - i) % 8], piece_s.at[i - 1], piece_r.at[i - 1],
                near_xc[i - 1]).wait_recv()
     block[...] = jnp.concatenate(
         [pieces[t].astype(F32)[0:6] for t in range(8)], axis=0).astype(BF)
@@ -294,8 +358,8 @@
         pass_rows(2, g)
         pass_columns(2, g, (0,))
     for c in range(GROUPS):
-        rows_then_columns(0, c)
-        rows_then_columns(1, c)
+        if c in (0, 2):
+            all_rows_then_columns(c // 2)
         ring_relay(c, 1)
         core_copy(c, 1).start()
         core_copy(c, 3).start()
@@ -314,7 +378,8 @@
         columns(3, c, 0)
         pass_columns(0, c, (-1, 1))
         pass_columns(1, c, (-1, 1))
-        rows_then_columns(2, c)
+        if c == 1:
+            all_rows_then_columns(2)
 
     lane = lax.broadcasted_iota(jnp.int32, (1, CELLS), 1)
     slot, token = lane // TOK, lane % TOK
@@ -335,24 +400,38 @@
     lane_of = lax.broadcasted_iota(jnp.int32, (TOK, TOK), 1)
 
     def forward(g, found):
-        all_columns(0, g)
-        all_columns(1, g)
         for i in range(PER):
             h = g * PER + i
-            s = nt(qn[h, OWN], kn[h].reshape(CELLS, HD)) * FACTOR + window(h, key_bias)
+            p = place_ref[h]
+            s = nt(natural[2, h], kn[p].reshape(CELLS, HD)) * FACTOR + window(h, key_bias)
             top = jnp.max(s, axis=1, keepdims=True)
-            p = jnp.exp(s - top)
-            summed = jnp.sum(p, axis=1, keepdims=True)
-            w = (p * (1.0 / summed)).astype(BF)
+            e = jnp.exp(s - top)
+            summed = jnp.sum(e, axis=1, keepdims=True)
+            w = (e * (1.0 / summed)).astype(BF)
             probs[h] = w
-            o = nn(w, vn[h].reshape(CELLS, HD)).astype(BF)
+            o = nn(w, vn[p].reshape(CELLS, HD)).astype(BF)
             att[g, :, i * HD:(i + 1) * HD] = o
             correction = jnp.sum(o.astype(F32) * dn[h, OWN].astype(F32), axis=1, keepdims=True)
             found = jnp.where(lane_of == h, top + jnp.log(summed), found)
             found = jnp.where(lane_of == HEADS + h, correction, found)
         return found
 
-    found = lax.fori_loop(0, GROUPS, forward, jnp.zeros((TOK, TOK), F32))
+    for g in RELAYED:
+        pass_rows(3, g)
+        pass_columns(3, g, (0,))
+    for g in range(GROUPS):
+        all_columns(0, g)
+        all_columns(1, g)
+    found = forward(0, jnp.zeros((TOK, TOK), F32))
+    for g in RELAYED:
+        pass_columns(2, g, (-1, 1))
+    rows_then_columns(3, 0)
+    rows_then_columns(3, 1)
+    found = forward(1, found)
+    rows_then_columns(3, 2)
+    rows_then_columns(3, 3)
+    found = forward(2, found)
+    found = forward(3, found)
     own_stats[...] = found
     stats[OWN] = found.T
 
@@ -365,11 +444,7 @@
     stat(7, OWN, west).start()
 
     for g in RELAYED:
-        pass_rows(3, g)
-        pass_columns(3, g, (0,))
-        pass_columns(2, g, (-1, 1))
-    for g in range(GROUPS):
-        rows_then_columns(3, g)
+        pass_columns(3, g, (-1, 1))
 
     for s in range(SLABS):
         total = jnp.zeros((TOK, SLABW), F32)
@@ -388,33 +463,34 @@
         for i in range(PER):
             h = g * PER + i
             correction = jnp.sum(jnp.where(lane_of == HEADS + h, own_stats[...], 0.0), axis=1, keepdims=True)
-            dp = nt(dn[h, OWN], vn[h].reshape(CELLS, HD))
+            p = place_ref[h]
+            dp = nt(dn[h, OWN], vn[p].reshape(CELLS, HD))
             ds = (probs[h].astype(F32) * (dp - correction)).astype(BF)
-            dq = nn(ds, kn[h].reshape(CELLS, HD)) * FACTOR
+            dq = nn(ds, kn[p].reshape(CELLS, HD)) * FACTOR
             dq_ref[:, pl.ds(pl.multiple_of(h * HD, HD), HD)] = dq.astype(BF)
         return carry
 
     lax.fori_loop(0, GROUPS, query_part, 0)
 
-    for g in range(GROUPS):
-        pass_columns(3, g, (-1, 1))
     for slot in (0, 1, 2, 6, 7, 8):
         stat(slot, OWN, east).wait_recv()
     cell = lax.broadcasted_iota(jnp.int32, (TOK, 1), 0)
     own_ok = (th * 8 + (cell // 8) % 8 < limit_rows) & (tw * 8 + cell % 8 < limit_cols)
 
+    for g in range(GROUPS):
+        all_columns(2, g)
+
     def key_part(g, carry):
-        all_columns(2, g)
         all_columns(3, g)
         for i in range(PER):
             h = g * PER + i
             totals = jnp.concatenate([stats[j, pl.ds(h, 1)] for j in range(9)], axis=1)
             corrections = jnp.concatenate([stats[j, pl.ds(HEADS + h, 1)] for j in range(9)], axis=1)
             shift = window(h, query_bias) - totals
-            qs = qn[h].reshape(CELLS, HD)
+            qs = qn[place_ref[h]].reshape(CELLS, HD)
             ds_near = dn[h].reshape(CELLS, HD)
-            w = jnp.exp(nt(kn[h, OWN], qs) * FACTOR + shift)
-            dp = nt(vn[h, OWN], ds_near)
+            w = jnp.exp(nt(natural[0, h], qs) * FACTOR + shift)
+            dp = nt(natural[1, h], ds_near)
             ds = (w * (dp - corrections)).astype(BF)
             dk = jnp.where(own_ok, nn(ds, qs) * FACTOR, 0.0)
             dv = jnp.where(own_ok, nn(w.astype(BF), ds_near), 0.0)
@@ -426,7 +502,7 @@
     lax.fori_loop(0, GROUPS, key_part, 0)
 
     for i in range(1, 8):
-        remote(w_hbm.at[0], pieces.at[0], piece_s.at[i - 1], piece_r.at[i - 1], near_xc[i - 1]).wait_send()
+        remote(padded.at[0], pieces.at[0], piece_s.at[i - 1], piece_r.at[i - 1], near_xc[i - 1]).wait_send()
         remote(block, z_place(z), z_s.at[i - 1], z_r.at[i - 1], near_z[i - 1]).wait_send()
     for c in range(GROUPS):
         for stage in range(2):
@@ -453,23 +529,19 @@
                 @pl.when(first_col | last_col)
                 def _():
                     for dr in (-1, 0, 1):
-                        col_pass(number, g, dr, OWN, north).wait_send()
+                        col_pass(number, g, dr, 1 + dr, north).wait_send()
     for slot in (0, 1, 2, 3, 5, 6, 7, 8):
         stat(slot, OWN, east).wait_send()
 
 
-def on_device(q, k, v, out_grad, out_weight, extent, pad):
-    shape = q.shape
-    flat = lambda a: a.reshape(TOK, a.shape[-1])
-    pieces = out_weight.reshape(6, SLABS, SLABW).transpose(1, 0, 2)
-    pieces = jnp.pad(pieces, ((0, 0), (0, 10), (0, 0)))
+def run(number, q, k, v, out_grad, pieces, extent, pad):
     hbm = pl.BlockSpec(memory_space=pl.ANY)
     smem = pl.BlockSpec(memory_space=pltpu.SMEM)
     vmem = pl.BlockSpec(memory_space=pltpu.VMEM)
     near = pltpu.VMEM((HEADS, 9, TOK, HD), BF)
     dma = pltpu.SemaphoreType.DMA
-    out, dq, dk, dv = pl.pallas_call(
-        kernel,
+    return pl.pallas_call(
+        functools.partial(kernel, SIZES[number]),
         out_shape=(
             jax.ShapeDtypeStruct((TOK, D), BF),
             jax.ShapeDtypeStruct((TOK, E), BF),
@@ -488,7 +560,6 @@
             pltpu.VMEM((HEADS, TOK, CELLS), BF),
             pltpu.VMEM((TOK, TOK), F32),
             pltpu.VMEM((9, TOK, TOK), F32),
-            pltpu.VMEM((16, 128), BF),
             dma((4, HEADS)),
             dma((7,)), dma((7,)), dma((7,)), dma((7,)),
             dma((GROUPS, 2, 4)), dma((GROUPS, 2, 4)),
@@ -497,12 +568,36 @@
             dma((9,)), dma((9,)),
             pltpu.VMEM((4, 2, PER, TOK, HD), BF),
             pltpu.VMEM((4, 2, 3, PER, TOK, HD), BF),
+            pltpu.VMEM((3, HEADS, TOK, HD), BF),
+            pltpu.SMEM((HEADS,), jnp.int32),
+            pltpu.VMEM((8, 16, SLABW), BF),
             dma((4, 2)), dma((4, 2)), dma((4, 2, 3)), dma((4, 2, 3)),
         ],
         compiler_params=pltpu.CompilerParams(
-            collective_id=0, has_side_effects=True, vmem_limit_bytes=60 * 1024 * 1024),
+            collective_id=number, has_side_effects=True, vmem_limit_bytes=60 * 1024 * 1024),
         cost_estimate=pl.CostEstimate(flops=7 * 10**9, bytes_accessed=6 * 10**6, transcendentals=4 * 10**6),
-    )(extent, pad, flat(q), flat(k), flat(v), flat(out_grad), pieces)
+    )(extent, pad, q, k, v, out_grad, pieces)
+
+
+def choice(extent):
+    in_rows, in_cols = extent[0], extent[1]
+    both = jnp.sum(in_rows * in_cols)
+    rows_only, cols_only = jnp.sum(in_rows) - both, jnp.sum(in_cols) - both
+    number = jnp.int32(len(SIZES) - 1)
+    for i in reversed(range(len(SIZES) - 1)):
+        n_rows, n_cols, n_both = SIZES[i]
+        beyond = jnp.maximum(rows_only - (n_rows - n_both), 0) + jnp.maximum(cols_only - (n_cols - n_both), 0)
+        number = jnp.where(beyond + both <= n_both, i, number)
+    return number
+
+
+def on_device(q, k, v, out_grad, out_weight, extent, pad):
+    shape = q.shape
+    flat = lambda a: a.reshape(TOK, a.shape[-1])
+    pieces = out_weight.reshape(6, SLABS, SLABW).transpose(1, 0, 2)
+    out, dq, dk, dv = lax.switch(
+        choice(extent), [functools.partial(run, i) for i in range(len(SIZES))],
+        flat(q), flat(k), flat(v), flat(out_grad), pieces, extent, pad)
     return (out.reshape(out_grad.shape), dq.reshape(shape), dk.reshape(shape), dv.reshape(shape))
 
 

time: 137 us -> 120 us (0.88)
  the two profiles are of different devices: /device:TPU:32 before, /device:TPU:1 now
where the time goes in v3:
time: 120 us; the launch traced here: 117 us
  Pallas kernels  107 us (89%)
  between operations  4.55 us (4%)
  local copies, waits for them, and re-layouts  4.44 us (4%)
    pallas_call x1, Pallas kernels, run(): pl.pallas_call(functools.partial(kernel, SIZES[number]), out_shape=(jax.S...  107 us
    unnamed x8, local copies, waits for them, and re-layouts  4.44 us

profile of v3, /device:TPU:1, one launch (start us, length us, event | category | flops | bytes accessed | tf_op | source)
XLA Modules:
  0.0 117.3 jit_solution(9062499020095984578)
XLA Ops:
  0.6 0.0 copy-start
  0.6 0.7 copy-done
  1.3 0.7 slice_reduce_fusion
  5.9 0.0 copy-start.1
  5.9 0.6 copy-done.1
  6.5 107.6 %conditional.1 = ((bf16[128,3072]{1,0:T(8,128)(2,1)S(1)}, bf16[128,1536]{1,0:T(8,128)(2,1)S(1)}, bf16[128,1536]{1,0:T(8,128)(2,1)S(1)}, bf16[128,1536]{1,0:T(8,128)(2,1)S(1)})) conditional(s32[]{:T(128)} %clamp.3, (s32[2,12]{1,0:T(2,128)S(1)}, s32[2]{0:T(128)S(1)}, bf16[128,1536]{1,0:T(8,128)(2,1)}, bf16[128,1536]{1,0:T(8,128)(2,1)}, ...), branch_computations={%region_3.4_spmd, %region_4.5_spmd, %region_5.6_spmd} | conditional | flops 7000000000 | bytes 6000008 | solution.py:598
  6.5 107.0 %branch_0_fun.1 = (bf16[128,3072]{1,0:T(8,128)(2,1)S(1)}, bf16[128,1536]{1,0:T(8,128)(2,1)S(1)}, bf16[128,1536]{1,0:T(8,128)(2,1)S(1)}, bf16[128,1536]{1,0:T(8,128)(2,1)S(1)}) custom-call(s32[2,12]{1,0:T(2,128)S(1)} %get-tuple-element.58.ext_ref, s32[2]{0:T(128)S(1)} %get-tuple-element.59.pad_ref, bf16[128,1536]{1,0:T(8,128)(2,1)} %get-tuple-element.60.q_hbm, ...), custom_call_target="tpu_custom_call" | custom-call | flops 7000000000 | bytes 6000000 | tf_op jit(solution)/shard_map/cond/branch_0_fun/pallas_call | solution.py:543
  114.2 0.9 copy.27
  115.1 0.7 copy.28
  115.8 0.7 copy.29
  116.6 0.7 copy.30
Async XLA Ops:
  0.6 0.7 copy-start
  5.9 0.7 copy-start.1

commit v4 on v3

--- a/solution.py
+++ b/solution.py
@@ -64,7 +64,8 @@
         )
 
     barrier = pltpu.get_barrier_semaphore()
-    greeted = [north, south, west, east] + near_xc + near_z + near_y
+    corners = [tile(-1, -1), tile(-1, 1), tile(1, -1), tile(1, 1)]
+    greeted = [north, south, west, east] + near_xc + near_z + near_y + corners
     for target in greeted:
         pl.semaphore_signal(barrier, inc=1, device_id=target, device_id_type=MESH)
     loads = []
@@ -376,8 +377,9 @@
             dn[c * PER + i, OWN] = total[:, i * HD:(i + 1) * HD].astype(BF)
         rows(3, c)
         columns(3, c, 0)
-        pass_columns(0, c, (-1, 1))
-        pass_columns(1, c, (-1, 1))
+        if c < 2:
+            for g in RELAYED:
+                pass_columns(c, g, (-1, 1))
         if c == 1:
             all_rows_then_columns(2)
 
@@ -433,15 +435,16 @@
     found = forward(2, found)
     found = forward(3, found)
     own_stats[...] = found
-    stats[OWN] = found.T
-
-    def stat(slot, source, device):
-        return remote(stats.at[source], stats.at[slot], stat_s.at[slot], stat_r.at[slot], device)
-
-    stat(3, OWN, south).start()
-    stat(5, OWN, north).start()
-    stat(1, OWN, east).start()
-    stat(7, OWN, west).start()
+    stats[OWN] = found.T[0:2 * HEADS]
+
+    around = [(a, b) for a in (-1, 0, 1) for b in (-1, 0, 1) if (a, b) != (0, 0)]
+
+    def stat(a, b):
+        j = (b + 1) * 3 + a + 1
+        return remote(stats.at[OWN], stats.at[j], stat_s.at[j], stat_r.at[j], tile(-a, -b))
+
+    for a, b in around:
+        stat(a, b).start()
 
     for g in RELAYED:
         pass_columns(3, g, (-1, 1))
@@ -451,13 +454,6 @@
         for c in range(GROUPS):
             total += nn(att[c], wb[c, s // 4, s % 4].reshape(PER * HD, SLABW))
         out_ref[:, s * SLABW:(s + 1) * SLABW] = total.astype(BF)
-
-    stat(3, OWN, south).wait_recv()
-    stat(0, 3, east).start()
-    stat(6, 3, west).start()
-    stat(5, OWN, north).wait_recv()
-    stat(2, 5, east).start()
-    stat(8, 5, west).start()
 
     def query_part(g, carry):
         for i in range(PER):
@@ -472,8 +468,8 @@
 
     lax.fori_loop(0, GROUPS, query_part, 0)
 
-    for slot in (0, 1, 2, 6, 7, 8):
-        stat(slot, OWN, east).wait_recv()
+    for a, b in around:
+        stat(a, b).wait_recv()
     cell = lax.broadcasted_iota(jnp.int32, (TOK, 1), 0)
     own_ok = (th * 8 + (cell // 8) % 8 < limit_rows) & (tw * 8 + cell % 8 < limit_cols)
 
@@ -530,8 +526,8 @@
                 def _():
                     for dr in (-1, 0, 1):
                         col_pass(number, g, dr, 1 + dr, north).wait_send()
-    for slot in (0, 1, 2, 3, 5, 6, 7, 8):
-        stat(slot, OWN, east).wait_send()
+    for a, b in around:
+        stat(a, b).wait_send()
 
 
 def run(number, q, k, v, out_grad, pieces, extent, pad):
@@ -559,7 +555,7 @@
             pltpu.VMEM((GROUPS, TOK, PER * HD), BF),
             pltpu.VMEM((HEADS, TOK, CELLS), BF),
             pltpu.VMEM((TOK, TOK), F32),
-            pltpu.VMEM((9, TOK, TOK), F32),
+            pltpu.VMEM((9, 2 * HEADS, TOK), F32),
             dma((4, HEADS)),
             dma((7,)), dma((7,)), dma((7,)), dma((7,)),
             dma((GROUPS, 2, 4)), dma((GROUPS, 2, 4)),
@@ -579,16 +575,30 @@
     )(extent, pad, q, k, v, out_grad, pieces)
 
 
-def choice(extent):
-    in_rows, in_cols = extent[0], extent[1]
-    both = jnp.sum(in_rows * in_cols)
-    rows_only, cols_only = jnp.sum(in_rows) - both, jnp.sum(in_cols) - both
+def choose(ext_ref, number_ref):
+    both = rows_only = cols_only = jnp.int32(0)
+    for h in range(HEADS):
+        in_rows, in_cols = ext_ref[0, h], ext_ref[1, h]
+        both += in_rows * in_cols
+        rows_only += in_rows * (1 - in_cols)
+        cols_only += in_cols * (1 - in_rows)
     number = jnp.int32(len(SIZES) - 1)
     for i in reversed(range(len(SIZES) - 1)):
         n_rows, n_cols, n_both = SIZES[i]
         beyond = jnp.maximum(rows_only - (n_rows - n_both), 0) + jnp.maximum(cols_only - (n_cols - n_both), 0)
         number = jnp.where(beyond + both <= n_both, i, number)
-    return number
+    number_ref[0] = number
+
+
+def choice(extent):
+    smem = pl.BlockSpec(memory_space=pltpu.SMEM)
+    number = pl.pallas_call(
+        choose,
+        out_shape=jax.ShapeDtypeStruct((1,), jnp.int32),
+        in_specs=[smem],
+        out_specs=smem,
+    )(extent)
+    return number[0]
 
 
 def on_device(q, k, v, out_grad, out_weight, extent, pad):

time: 120 us -> 114 us (0.950); the launches traced: 117 us -> 114 us
  between operations: 4.55 us -> 1.31 us
    pallas_call x0 -> x1, Pallas kernels: none -> 1.24 us  [choice(): pl.pallas_call(choose, out_shape=jax.ShapeDtypeStruct((1,), jnp.int32), i...]
where the time goes in v4:
time: 114 us
  Pallas kernels  108 us (95%)
  local copies, waits for them, and re-layouts  3.79 us (3%)
  between operations  1.31 us (1%)
    pallas_call x1, Pallas kernels, run(): pl.pallas_call(functools.partial(kernel, SIZES[number]), out_shape=(jax.S...  107 us
    unnamed x8, local copies, waits for them, and re-layouts  3.79 us

profile of v4, /device:TPU:1, one launch (start us, length us, event | category | flops | bytes accessed | tf_op | source)
XLA Modules:
  0.0 113.8 jit_solution(384263238903524206)
XLA Ops:
  0.6 1.2 %shard_map.102 = s32[1]{0:T(128)} custom-call(s32[2,12]{1,0:T(2,128)} %ext_ref.1), custom_call_target="tpu_custom_call" | custom-call | tf_op jit(solution)/shard_map/pallas_call | solution.py:595
  2.5 0.0 copy-start
  2.5 0.0 copy-start.1
  2.6 0.7 copy-done
  3.2 0.0 copy-done.1
  3.2 107.4 %conditional.1 = ((bf16[128,3072]{1,0:T(8,128)(2,1)S(1)}, bf16[128,1536]{1,0:T(8,128)(2,1)S(1)}, bf16[128,1536]{1,0:T(8,128)(2,1)S(1)}, bf16[128,1536]{1,0:T(8,128)(2,1)S(1)})) conditional(s32[]{:T(128)} %bitcast, (s32[2,12]{1,0:T(2,128)S(1)}, s32[2]{0:T(128)S(1)}, bf16[128,1536]{1,0:T(8,128)(2,1)}, bf16[128,1536]{1,0:T(8,128)(2,1)}, ...), branch_computations={%region_0.0_spmd, %region_1.0_spmd, %region_2.0_spmd} | conditional | flops 7000000000 | bytes 6000008 | solution.py:608
  3.2 106.8 %branch_0_fun.1 = (bf16[128,3072]{1,0:T(8,128)(2,1)S(1)}, bf16[128,1536]{1,0:T(8,128)(2,1)S(1)}, bf16[128,1536]{1,0:T(8,128)(2,1)S(1)}, bf16[128,1536]{1,0:T(8,128)(2,1)S(1)}) custom-call(s32[2,12]{1,0:T(2,128)S(1)} %get-tuple-element.58.ext_ref, s32[2]{0:T(128)S(1)} %get-tuple-element.59.pad_ref, bf16[128,1536]{1,0:T(8,128)(2,1)} %get-tuple-element.60.q_hbm, ...), custom_call_target="tpu_custom_call" | custom-call | flops 7000000000 | bytes 6000000 | tf_op jit(solution)/shard_map/cond/branch_0_fun/pallas_call | solution.py:539
  110.6 0.9 copy.27
  111.5 0.7 copy.28
  112.3 0.7 copy.29
  113.0 0.7 copy.30
Async XLA Ops:
  2.5 0.7 copy-start
  2.5 0.7 copy-start.1

commit v5 on v4

--- a/solution.py
+++ b/solution.py
@@ -18,7 +18,7 @@
 ORDER = (2, 3, 0, 1)
 Y_FIRST = (1, 3)
 CELLS = 9 * TOK
-SIZES = ((9, 7, 4), (9, 9, 6), (12, 12, 12))
+SIZES = ((9, 8, 5), (12, 12, 12))
 MASKED = -1e30
 FACTOR = HD ** (-0.5)
 BF, F32 = jnp.bfloat16, jnp.float32

time: 114 us -> 114 us (level)
  no operation moved by 1% of the time
where the time goes in v5:
time: 114 us
  Pallas kernels  108 us (95%)
  local copies, waits for them, and re-layouts  3.79 us (3%)
  between operations  1.31 us (1%)
    pallas_call x1, Pallas kernels, run(): pl.pallas_call(functools.partial(kernel, SIZES[number]), out_shape=(jax.S...  107 us
    unnamed x8, local copies, waits for them, and re-layouts  3.79 us

profile of v5, /device:TPU:1, one launch (start us, length us, event | category | flops | bytes accessed | tf_op | source)
XLA Modules:
  0.0 114.0 jit_solution(5348784435735296973)
XLA Ops:
  0.6 1.2 %shard_map.102 = s32[1]{0:T(128)} custom-call(s32[2,12]{1,0:T(2,128)} %ext_ref.1), custom_call_target="tpu_custom_call" | custom-call | tf_op jit(solution)/shard_map/pallas_call | solution.py:595
  2.5 0.0 copy-start
  2.5 0.0 copy-start.1
  2.6 0.7 copy-done
  3.2 0.0 copy-done.1
  3.2 107.7 %conditional.1 = ((bf16[128,3072]{1,0:T(8,128)(2,1)S(1)}, bf16[128,1536]{1,0:T(8,128)(2,1)S(1)}, bf16[128,1536]{1,0:T(8,128)(2,1)S(1)}, bf16[128,1536]{1,0:T(8,128)(2,1)S(1)})) conditional(s32[]{:T(128)} %bitcast, (s32[2,12]{1,0:T(2,128)S(1)}, s32[2]{0:T(128)S(1)}, bf16[128,1536]{1,0:T(8,128)(2,1)}, bf16[128,1536]{1,0:T(8,128)(2,1)}, ...), branch_computations={%region_0.0_spmd, %region_1.0_spmd} | conditional | flops 7000000000 | bytes 6000008 | solution.py:608
  3.2 107.1 %branch_0_fun.1 = (bf16[128,3072]{1,0:T(8,128)(2,1)S(1)}, bf16[128,1536]{1,0:T(8,128)(2,1)S(1)}, bf16[128,1536]{1,0:T(8,128)(2,1)S(1)}, bf16[128,1536]{1,0:T(8,128)(2,1)S(1)}) custom-call(s32[2,12]{1,0:T(2,128)S(1)} %get-tuple-element.40.ext_ref, s32[2]{0:T(128)S(1)} %get-tuple-element.41.pad_ref, bf16[128,1536]{1,0:T(8,128)(2,1)} %get-tuple-element.42.q_hbm, ...), custom_call_target="tpu_custom_call" | custom-call | flops 7000000000 | bytes 6000000 | tf_op jit(solution)/shard_map/cond/branch_0_fun/pallas_call | solution.py:539
  110.9 0.9 copy.23
  111.8 0.7 copy.24
  112.5 0.7 copy.25
  113.3 0.7 copy.26
Async XLA Ops:
  2.5 0.7 copy-start
  2.5 0.7 copy-start.1
